TPU v7x, 32 devices: a whole 2x2x4 slice. The times are simulated.
32 devices in a mesh: ma: 2 (over y), an: 16 (over z, x, core).
Axes of the slice: x: 2, y: 2, z: 4, core: 2. Of those that a mesh axis runs over, the one named last changes fastest.
Arguments:
- tokens: bfloat16 [64, 512, 768], P(('ma', 'an')), may hold values from -6 to 6
- tasks: int32 [64], P(('ma', 'an')), may hold values from 0 to 7
- segments: int32 [64, 512], P(('ma', 'an')), may hold values from 0 to 3, never falling along the last dimension, each value on 1 to 256 neighbouring positions
- buckets: int32 [1023], replicated, may hold values from 0 to 31
- w_query: bfloat16 [768, 768], replicated, may hold values from -0.21875 to 0.21875
- w_key: bfloat16 [768, 768], replicated, may hold values from -0.21875 to 0.21875
- w_value: bfloat16 [768, 768], replicated, may hold values from -0.21875 to 0.21875
- w_out: bfloat16 [768, 768], replicated, may hold values from -1.75 to 1.75
- w_up: bfloat16 [768, 3072], P('ma', 'an'), may hold values from -0.21875 to 0.21875
- w_down: bfloat16 [3072, 768], P('an', 'ma'), may hold values from -0.109375 to 0.109375
- bias_table: float32 [8, 32, 12], replicated, may hold values from -6 to 6
- gain_attn: float32 [768], replicated, may hold values from 0.5 to 1.5
- gain_ffn: float32 [768], replicated, may hold values from 0.5 to 1.5
- cotangent: bfloat16 [64, 512, 768], P(('ma', 'an')), may hold values from -6 to 6
Outputs:
- output: bfloat16 [64, 512, 768], P(('ma', 'an'))
- grad_tokens: float32 [64, 512, 768], P(('ma', 'an'))
- grad_query: float32 [768, 768], replicated
- grad_key: float32 [768, 768], replicated
- grad_value: float32 [768, 768], replicated
- grad_w_out: float32 [768, 768], replicated
- grad_up: float32 [768, 3072], P('ma', 'an')
- grad_down: float32 [3072, 768], P('an', 'ma')
- grad_table: float32 [8, 32, 12], replicated
- grad_gain_attn: float32 [768], replicated
- grad_gain_ffn: float32 [768], replicated
Inputs may be any that keep to these rules, and one draw needn't show every extreme that they name: `segments`: within a row segment numbers never fall; a token attends only to tokens of its own segment.
All inputs are finite; a program needn't handle non-finite values.
Results may differ from a plain program's by a relative error of at most 0.015.
Values may be sent and summed in bfloat16 or wider, within the bound.
No kernel may reach another device: no remote copies, remote signals or barrier semaphores. Data moves between devices by JAX's collectives and lax.ppermute only.
A program may use at most 256 MiB of HBM per device.

v0:
```python
import jax
import jax.numpy as jnp
from jax import lax
from jax.sharding import PartitionSpec as P
from jax.experimental import pallas as pl
from jax.experimental.pallas import tpu as pltpu

epsilon = 1e-06
highest = lax.Precision.HIGHEST
F32 = jnp.float32
BF16 = jnp.bfloat16
BLOCK = 128
REACH = 2
WIDE = 6 * BLOCK
CONTRACT_LANES = (((1,), (1,)), ((), ()))
CONTRACT_ROWS = (((0,), (0,)), ((), ()))
PLAIN = (((1,), (0,)), ((), ()))
hold = lax.optimization_barrier
brief = pl.CostEstimate(flops=1000, bytes_accessed=1000, transcendentals=0)


def far(x):
    return pltpu.with_memory_space_constraint(x, pltpu.HBM)


def dot(a, b, dims=PLAIN):
    return lax.dot_general(a, b, dims, preferred_element_type=F32)


def attend_body(p_ref, kseg_ref, qseg_ref, f_ref, *refs):
    u_ref, s_ref, o_ref, ot_ref = refs[-4:]
    length = p_ref.shape[0]
    blocks = length // BLOCK
    lane = lax.broadcasted_iota(jnp.int32, (length, BLOCK), 1)
    q_aug = jnp.concatenate([p_ref[:, :BLOCK] * BF16(0.125), qseg_ref[...]], axis=1)
    k = p_ref[:, BLOCK : 2 * BLOCK]
    v_t = p_ref[:, 2 * BLOCK :].astype(F32).T.astype(BF16)
    k_aug = [
        jnp.concatenate([jnp.where((lane >= 64) == (h == 1), k, BF16(0)), kseg_ref[...]], axis=1)
        for h in range(2)
    ]
    v_aug = [
        jnp.concatenate([v_t[64 * h : 64 * h + 64], jnp.ones((16, length), BF16)], axis=0)
        for h in range(2)
    ]
    tiles = [
        pltpu.roll(
            jnp.broadcast_to(f_ref[0, h : h + 1, :], (BLOCK, WIDE)), 0, 1, stride=1, stride_axis=0
        )
        for h in range(2)
    ]

    def score(h, s):
        return dot(k_aug[h], q_aug[256 * s : 256 * s + 256], CONTRACT_LANES)

    def weigh(h, s, st):
        for half in range(2):
            qb = 2 * s + half
            scored = {}
            peak = None
            for kb in range(blocks):
                o = kb - qb
                if abs(o) > REACH:
                    continue
                b = (
                    st[BLOCK * kb : BLOCK * kb + BLOCK, BLOCK * half : BLOCK * half + BLOCK]
                    + tiles[h][:, 384 - BLOCK * o : 512 - BLOCK * o]
                )
                scored[kb] = b
                peak = b if peak is None else jnp.maximum(peak, b)
            peak = jnp.max(peak, axis=0, keepdims=True)
            for kb in range(blocks):
                if kb in scored:
                    e = jnp.exp(scored[kb] - peak).astype(BF16)
                else:
                    e = jnp.zeros((BLOCK, BLOCK), BF16)
                u_ref[0, h, BLOCK * kb : BLOCK * kb + BLOCK, BLOCK * qb : BLOCK * qb + BLOCK] = e

    def mix(h, s):
        ot = dot(v_aug[h], u_ref[0, h, :, 256 * s : 256 * s + 256])
        r = 1.0 / ot[64:65]
        s_ref[0, h : h + 1, 256 * s : 256 * s + 256] = r
        return ot[:64] * r

    units = [(h, s) for h in range(2) for s in range(blocks // 2)]
    made = {}
    ahead = score(*units[0])
    for i, unit in enumerate(units):
        st = ahead
        if i + 1 < len(units):
            ahead = score(*units[i + 1])
        weigh(*unit, st)
        if i > 0:
            made[units[i - 1]] = mix(*units[i - 1])
    made[units[-1]] = mix(*units[-1])
    outs = [
        jnp.concatenate([made[h, s] for s in range(blocks // 2)], axis=1) for h in range(2)
    ]
    o_t = jnp.concatenate(outs, axis=0)
    o_ref[...] = o_t.T.astype(BF16)
    ot_ref[...] = o_t.astype(BF16)


def pair_spec(length, per_group, first):
    return pl.BlockSpec(
        (None, length, 3 * BLOCK),
        lambda p, r: ((first + p) // per_group, r, (first + p) % per_group),
    )


def attend(first, count, pairs, rows, length, proj, kseg, qseg, bias, made):
    steps = rows * pairs
    args = [far(proj), kseg, qseg, bias]
    specs = [
        pair_spec(length, pairs // proj.shape[0], first),
        pl.BlockSpec((length, BLOCK), lambda p, r: (r, 0)),
        pl.BlockSpec((length, BLOCK), lambda p, r: (r, 0)),
        pl.BlockSpec((1, 2, WIDE), lambda p, r: (r * pairs + first + p, 0, 0)),
    ]
    alias = {}
    if made is not None:
        alias = {len(args) + i: i for i in range(4)}
        args += [far(made[0]), made[1], made[2], made[3]]
        specs += [pl.BlockSpec(memory_space=pl.ANY)] * 4
    return pl.pallas_call(
        attend_body,
        grid=(count, rows),
        in_specs=specs,
        out_specs=[
            pl.BlockSpec((1, 2, length, length), lambda p, r: ((first + p) * rows + r, 0, 0, 0)),
            pl.BlockSpec((1, 2, length), lambda p, r: ((first + p) * rows + r, 0, 0)),
            pl.BlockSpec((length, BLOCK), lambda p, r: (r, first + p)),
            pl.BlockSpec((BLOCK, length), lambda p, r: (first + p, r)),
        ],
        out_shape=[
            pltpu.HBM((steps, 2, length, length), BF16),
            jax.ShapeDtypeStruct((steps, 2, length), F32),
            jax.ShapeDtypeStruct((rows * length, pairs * BLOCK), BF16),
            jax.ShapeDtypeStruct((pairs * BLOCK, rows * length), BF16),
        ],
        input_output_aliases=alias,
        compiler_params=pltpu.CompilerParams(vmem_limit_bytes=16 * 1024 * 1024),
        cost_estimate=brief,
        name="attend",
    )(*args)


def attend_grad_body(
    place_ref, p_ref, u_ref, s_ref, o_ref, g_ref, mine_ref, theirs_ref, *refs
):
    dp_ref, df_ref, go_ref, gx_ref, ds_ref, acc_ref = refs[-6:]
    length = p_ref.shape[0]
    blocks = length // BLOCK
    lane = lax.broadcasted_iota(jnp.int32, (length, BLOCK), 1)
    q = p_ref[:, :BLOCK] * BF16(0.125)
    k = p_ref[:, BLOCK : 2 * BLOCK]
    v = p_ref[:, 2 * BLOCK :]
    k_t = k.astype(F32).T.astype(BF16)
    inv = jnp.concatenate(
        [jnp.broadcast_to(s_ref[0, h : h + 1, :], (64, length)) for h in range(2)], axis=0
    ).T
    g = g_ref[...].astype(F32) * inv
    prod = g * o_ref[...].astype(F32)
    g_low = g.astype(BF16)
    prod_hi = prod.astype(BF16)
    prod_lo = (prod - prod_hi.astype(F32)).astype(BF16)
    row = lax.broadcasted_iota(jnp.int32, (2 * BLOCK, BLOCK), 0)
    col = lax.broadcasted_iota(jnp.int32, (2 * BLOCK, BLOCK), 1)
    pick = jnp.where((((row // 64) % 2) == (col // 2)) & (col < 4), -1.0, 0.0).astype(BF16)
    centre = dot(jnp.concatenate([prod_hi, prod_lo], axis=1), pick)
    centre_hi = centre.astype(BF16)
    centre_lo = (centre - centre_hi.astype(F32)).astype(BF16)
    g_aug = jnp.concatenate([g_low, jnp.where(lane % 2 == 0, centre_hi, centre_lo)], axis=1)
    zero = BF16(0)
    mine = [(lane >= 64) == (h == 1) for h in range(2)]
    v_aug = [
        jnp.concatenate(
            [jnp.where(mine[h], v, zero), jnp.where((lane // 2) == h, BF16(1), zero)], axis=1
        )
        for h in range(2)
    ]
    diag = [[None] * (2 * REACH + 1) for _ in range(2)]
    dq_t, dv, dk = [], [], []

    def score(h, s):
        return dot(v_aug[h], g_aug[256 * s : 256 * s + 256], CONTRACT_LANES)

    def weigh(h, s, dp):
        for half in range(2):
            qb = 2 * s + half
            for kb in range(blocks):
                o = kb - qb
                krows = slice(BLOCK * kb, BLOCK * kb + BLOCK)
                qcols = slice(BLOCK * qb, BLOCK * qb + BLOCK)
                if abs(o) > REACH:
                    ds_ref[h, krows, qcols] = jnp.zeros((BLOCK, BLOCK), BF16)
                    continue
                ds = (
                    u_ref[0, h, krows, qcols].astype(F32)
                    * dp[krows, BLOCK * half : BLOCK * half + BLOCK]
                )
                ds_ref[h, krows, qcols] = ds.astype(BF16)
                d = diag[h][o + REACH]
                diag[h][o + REACH] = ds if d is None else d + ds

    def values(h):
        dv.append(dot(u_ref[0, h], jnp.where(mine[h], g_low, zero)))

    def keys(h):
        dk.append(dot(ds_ref[h], jnp.where(mine[h], q, zero)))

    def queries(h):
        dq_t.append(dot(k_t[64 * h : 64 * h + 64], ds_ref[h]))

    def offsets(h):
        wide = jnp.concatenate([jnp.zeros((BLOCK, BLOCK), F32)] + diag[h][::-1], axis=1)
        step = BLOCK // 2
        while step:
            wide = wide[:step] + pltpu.roll(wide[step:], WIDE - step, 1)
            step //= 2
        df_ref[0, h : h + 1, :] = wide

    strips = range(blocks // 2)
    dps = [[score(h, s) for s in strips] for h in range(2)]
    values(0)
    for s in strips:
        weigh(0, s, dps[0][s])
    values(1)
    keys(0)
    queries(0)
    for s in strips:
        weigh(1, s, dps[1][s])
    offsets(0)
    keys(1)
    queries(1)
    offsets(1)
    dv = dv[0] + dv[1]
    dk = dk[0] + dk[1]
    dq = jnp.concatenate(dq_t, axis=0).T * 0.125
    d_all = jnp.concatenate([dq.astype(BF16), dk.astype(BF16), dv.astype(BF16)], axis=1)
    dp_ref[...] = d_all
    half = mine_ref.shape[0]
    row_step = pl.program_id(1)
    add = dot(jnp.concatenate([mine_ref[...], theirs_ref[...]], axis=0), d_all)

    @pl.when(row_step == 0)
    def _():
        acc_ref[...] = add

    @pl.when(row_step != 0)
    def _():
        acc_ref[...] += add

    @pl.when(row_step == pl.num_programs(1) - 1)
    def _():
        go_ref[...] = acc_ref[:half].astype(BF16)
        gx_ref[...] = acc_ref[half:].astype(BF16)


def attend_grad(
    net, first, count, pairs, rows, length, proj, made, grad_mixed, normed_t, cols, buffers, at
):
    saved, inverse, mixed, _ = made
    steps = rows * count
    half = normed_t.shape[0] // 2
    wide = 3 * BLOCK
    args = [far(proj), far(saved), inverse, mixed, grad_mixed, far(normed_t), far(normed_t)]
    specs = [
        pl.BlockSpec(
            (None, length, wide),
            lambda p, r, w, per=pairs // proj.shape[0]: ((first + p) // per, r, (first + p) % per),
        ),
        pl.BlockSpec((1, 2, length, length), lambda p, r, w: ((first + p) * rows + r, 0, 0, 0)),
        pl.BlockSpec((1, 2, length), lambda p, r, w: ((first + p) * rows + r, 0, 0)),
        pl.BlockSpec((length, BLOCK), lambda p, r, w: (r, first + p)),
        pl.BlockSpec((length, BLOCK), lambda p, r, w: (r, first + p)),
        pl.BlockSpec((half, length), lambda p, r, w: (w[3], r)),
        pl.BlockSpec((half, length), lambda p, r, w: (1 - w[3], r)),
    ]
    alias = {}
    if buffers is not None:
        alias = {1 + len(args) + i: 2 + i for i in range(2)}
        args += [far(b) for b in buffers]
        specs += [pl.BlockSpec(memory_space=pl.ANY)] * 2
    g_spec = pl.BlockSpec((half, wide), lambda p, r, w: (0, at // wide + p))
    return pl.pallas_call(
        attend_grad_body,
        grid_spec=pltpu.PrefetchScalarGridSpec(
            num_scalar_prefetch=1,
            grid=(count, rows),
            in_specs=specs,
            out_specs=[
                pl.BlockSpec((length, wide), lambda p, r, w: (r, p)),
                pl.BlockSpec((1, 2, WIDE), lambda p, r, w: (p * rows + r, 0, 0)),
                g_spec,
                g_spec,
            ],
            scratch_shapes=[
                pltpu.VMEM((2, length, length), BF16),
                pltpu.VMEM((2 * half, wide), F32),
            ],
        ),
        out_shape=[
            pltpu.HBM((rows * length, count * wide), BF16),
            jax.ShapeDtypeStruct((steps, 2, WIDE), F32),
            pltpu.HBM((half, cols), BF16),
            pltpu.HBM((half, cols), BF16),
        ],
        input_output_aliases=alias,
        compiler_params=pltpu.CompilerParams(vmem_limit_bytes=24 * 1024 * 1024),
        cost_estimate=brief,
        name="attend_grad",
    )(net.places(), *args)


def pick(options, index):
    out = options[0]
    for k in range(1, len(options)):
        out = jnp.where(index == k, options[k], out)
    return out


def by_distance(slices, at):
    n = len(slices)
    return [pick(slices, lax.rem(at - t + n, n)) for t in range(n)]


def in_order(pieces, at):
    n = len(pieces)
    return [pick(pieces, lax.rem(at - k + n, n)) for k in range(n)]


def by_flip(slices, at):
    return [pick(slices, lax.bitwise_xor(at, k)) for k in range(len(slices))]


def cut_rows(v, n):
    size = v.shape[0] // n
    return [v[size * k : size * k + size] for k in range(n)]


def cut_lanes(v, n):
    size = v.shape[-1] // n
    return [v[..., size * k : size * k + size] for k in range(n)]


def total(parts):
    out = parts[0].astype(F32)
    for p in parts[1:]:
        out = out + p.astype(F32)
    return out


class Links:
    def __init__(self, ma, an, width):
        z = min(4, an // 2)
        self.an = an
        self.size = {"y": ma, "z": z, "x": an // (2 * z), "c": 2}
        self.stride = {"c": 1, "x": 2, "z": 2 * self.size["x"]}
        self.tidy = width % (ma * BLOCK) == 0 and width % (8 * ma * an) == 0

    def places(self):
        an = lax.axis_index("an")
        found = [lax.axis_index("ma")]
        found += [(an // self.stride[a]) % self.size[a] for a in ("z", "x", "c")]
        return jnp.stack([f.astype(jnp.int32) for f in found])

    def fetch(self, value, axis, back):
        n = self.size[axis]
        if axis == "y":
            return lax.ppermute(value, "ma", [(i, (i + back) % n) for i in range(n)])
        s = self.stride[axis]
        pairs = []
        for i in range(self.an):
            at = (i // s) % n
            pairs.append((i, i + ((at + back) % n - at) * s))
        return lax.ppermute(value, "an", pairs)

    def flip(self, value, axis, bits):
        s = self.stride[axis]
        pairs = []
        for i in range(self.an):
            at = (i // s) % self.size[axis]
            pairs.append((i, i + ((at ^ bits) - at) * s))
        return lax.ppermute(value, "an", pairs)

    def gather(self, value, axis):
        return [value] + [self.fetch(value, axis, t) for t in range(1, self.size[axis])]

    def spread(self, parts, axis):
        n = self.size[axis]
        return [parts[0]] + [self.fetch(parts[t], axis, n - t) for t in range(1, n)]

    def step(self, fn, arrays, shapes, name, along, steps=1, away=False):
        arrays, along = hold((list(arrays), along))
        return hold((self.stage(fn, arrays, shapes, name, steps, away), along))

    def stage(self, fn, arrays, shapes, name, steps, away):
        outs = [jax.ShapeDtypeStruct(s, BF16) for s in shapes]
        place = self.places()
        if not self.tidy:
            got = fn(*[place[i] for i in range(4)], *arrays)
            return [g.astype(BF16).reshape(o.shape) for g, o in zip(got, outs)]
        count = len(arrays)

        def body(place_ref, *refs):
            got = fn(*[place_ref[i] for i in range(4)], *[r[...] for r in refs[:count]])
            for g, r in zip(got, refs[count:]):
                r[...] = g.astype(BF16)

        def spec(a):
            rest = len(a.shape) - 1
            return pl.BlockSpec(
                (a.shape[0] // steps,) + a.shape[1:], lambda i, p, rest=rest: (i,) + (0,) * rest
            )

        return pl.pallas_call(
            body,
            grid_spec=pltpu.PrefetchScalarGridSpec(
                num_scalar_prefetch=1,
                grid=(steps,),
                in_specs=[spec(a) for a in arrays],
                out_specs=[spec(o) for o in outs],
            ),
            out_shape=[pltpu.HBM(o.shape, o.dtype) for o in outs] if away else outs,
            compiler_params=pltpu.CompilerParams(vmem_limit_bytes=16 * 1024 * 1024),
            cost_estimate=brief,
            name=name,
        )(place, *arrays)


def gather_1(net, pieces, along):
    rows, cols = pieces[0].shape
    half = rows // 2
    n = len(pieces)

    def fn(y, z, x, c, *pieces):
        v = jnp.stack(in_order(pieces, z))
        return [v[:, :half], v[:, half:]]

    (a, b), along = net.step(fn, pieces, [(n, half, cols)] * 2, "gather_z", along)
    return (net.gather(a, "x"), net.gather(b, "y")), along


def gather_2(net, state, along):
    a, b = state
    n, half, cols = a[0].shape

    def fn(y, z, x, c, *parts):
        a_in = in_order(parts[: len(a)], x)
        b_in = in_order(parts[len(a) :], y)
        return [jnp.stack(a_in, axis=1), jnp.concatenate(b_in, axis=-1)]

    (a, b), along = net.step(
        fn, a + b, [(n, len(a), half, cols), (n, half, cols * len(b))], "gather_xy", along
    )
    return (net.gather(a, "y"), net.gather(b, "x")), along


def gather_3(net, state, along):
    a, b = state
    n, nx, half, cols = a[0].shape

    def fn(y, z, x, c, *parts):
        a_in = jnp.concatenate(in_order(parts[: len(a)], y), axis=-1)
        b_in = jnp.stack(in_order(parts[len(a) :], x), axis=1)
        return [jnp.concatenate([a_in, b_in], axis=2)]

    shape = (n, nx, 2 * half, cols * len(a))
    (own,), along = net.step(fn, a + b, [shape], "gather_yx", along, steps=n if net.tidy else 1)
    return net.gather(own, "c"), along


def scatter_1(net, own, theirs, along):
    nz, two, nx, hb, width = own.shape
    half = hb // 2
    ny = net.size["y"]

    def fn(y, z, x, c, own, theirs):
        v = total([own, theirs])
        a, b = v[..., :half, :], v[..., half:, :]
        return by_distance(cut_lanes(a, ny), y) + by_distance([b[:, :, k] for k in range(nx)], x)

    shapes = [(nz, two, nx, half, width // ny)] * ny + [(nz, two, half, width)] * nx
    parts, along = net.step(
        fn, [own, theirs], shapes, "scatter_yx", along, steps=nz if net.tidy else 1
    )
    return (net.spread(parts[:ny], "y"), net.spread(parts[ny:], "x")), along


def scatter_2(net, state, along):
    a, b = state
    nz, two, nx, half, cols = a[0].shape
    ny = net.size["y"]

    def fn(y, z, x, c, *parts):
        va, vb = total(parts[:ny]), total(parts[ny:])
        return by_distance([va[:, :, k] for k in range(nx)], x) + by_distance(cut_lanes(vb, ny), y)

    shapes = [(nz, two, half, cols)] * (nx + ny)
    parts, along = net.step(fn, a + b, shapes, "scatter_xy", along)
    return (net.spread(parts[:nx], "x"), net.spread(parts[nx:], "y")), along


def scatter_3(net, state, along):
    a, b = state
    nz, two, half, cols = a[0].shape

    def fn(y, z, x, c, *parts):
        v = jnp.concatenate([total(parts[: len(a)]), total(parts[len(a) :])], axis=2)
        return halves([v[k] for k in range(nz)], z)

    parts, along = net.step(fn, a + b, [(nz // 2, two, 2 * half, cols)] * 2, "scatter_z", along)
    return (parts[0], net.flip(parts[1], "z", 1)), along


def halves(slices, at):
    p = by_flip(slices, at)
    return [jnp.stack([p[0], p[2]]), jnp.stack([p[1], p[3]])]


def fold_z(net, state, along):
    kept, got = state

    def fn(y, z, x, c, kept, got):
        v = total([kept, got])
        return [v[0], v[1]]

    parts, along = net.step(fn, [kept, got], [kept.shape[1:]] * 2, "fold_z", along)
    return [parts[0], net.flip(parts[1], "z", 2)], along


def reduce_1(net, own, theirs, cut, along, away):
    rows, cols = own.shape
    ny, nx = net.size["y"], net.size["x"]

    def fn(y, z, x, c, own, theirs):
        v = total([own, theirs])
        return by_distance(cut_rows(v[:, :cut], ny), y) + by_distance(cut_rows(v[:, cut:], nx), x)

    shapes = [(rows // ny, cut)] * ny + [(rows // nx, cols - cut)] * nx
    parts, along = net.step(fn, [own, theirs], shapes, "reduce_yx", along, away=away)
    return (net.spread(parts[:ny], "y"), net.spread(parts[ny:], "x")), along


def reduce_2(net, state, along, away):
    a, b = state
    ny, nx = net.size["y"], net.size["x"]

    def fn(y, z, x, c, *parts):
        va, vb = total(parts[: len(a)]), total(parts[len(a) :])
        return by_distance(cut_rows(va, nx), x) + by_distance(cut_rows(vb, ny), y)

    shapes = [(a[0].shape[0] // nx, a[0].shape[1])] * nx
    shapes += [(b[0].shape[0] // ny, b[0].shape[1])] * ny
    parts, along = net.step(fn, a + b, shapes, "reduce_xy", along, away=away)
    return (net.spread(parts[:nx], "x"), net.spread(parts[nx:], "y")), along


def reduce_3(net, state, along):
    a, b = state
    n = net.size["z"]

    def fn(y, z, x, c, *parts):
        v = jnp.concatenate([total(parts[: len(a)]), total(parts[len(a) :])], axis=1)
        return halves(cut_rows(v, n), z)

    shape = (n // 2, a[0].shape[0] // n, a[0].shape[1] + b[0].shape[1])
    parts, along = net.step(fn, a + b, [shape] * 2, "reduce_z", along)
    return (parts[0], net.flip(parts[1], "z", 1)), along


def spread_0(net, parts, along):
    def fn(y, z, x, c, *parts):
        return [total(parts)]

    (front,), along = net.step(fn, parts, [parts[0].shape], "spread_sum", along)
    return [front, net.flip(front, "z", 2)], along


def spread_z(net, pieces, along):
    def fn(y, z, x, c, *pieces):
        return [jnp.stack(pieces)]

    (pair,), along = net.step(fn, pieces, [(2,) + pieces[0].shape], "spread_pair", along)
    return [pair, net.flip(pair, "z", 1)], along


def spread_1(net, pairs, cut, along):
    _, rows, cols = pairs[0].shape

    def fn(y, z, x, c, *pairs):
        found = [p[k].astype(F32) for k in range(2) for p in pairs]
        v = jnp.concatenate(by_flip(found, z), axis=0)
        return [v[:, :cut], v[:, cut:]]

    shapes = [(4 * rows, cut), (4 * rows, cols - cut)]
    (a, b), along = net.step(fn, pairs, shapes, "spread_z", along)
    return (net.gather(a, "x"), net.gather(b, "y")), along


def spread_2(net, state, along):
    a, b = state

    def fn(y, z, x, c, *parts):
        va = jnp.concatenate(in_order(parts[: len(a)], x), axis=0)
        vb = jnp.concatenate(in_order(parts[len(a) :], y), axis=0)
        return [va, vb]

    shapes = [(len(p) * p[0].shape[0], p[0].shape[1]) for p in (a, b)]
    (a, b), along = net.step(fn, a + b, shapes, "spread_xy", along)
    return (net.gather(a, "y"), net.gather(b, "x")), along


def spread_3(net, state, along):
    a, b = state

    def fn(y, z, x, c, *parts):
        va = jnp.concatenate(in_order(parts[: len(a)], y), axis=0)
        vb = jnp.concatenate(in_order(parts[len(a) :], x), axis=0)
        return [jnp.concatenate([va, vb], axis=1)]

    shape = (len(a) * a[0].shape[0], a[0].shape[1] + b[0].shape[1])
    (v,), along = net.step(fn, a + b, [shape], "spread_yx", along)
    return net.gather(v, "c"), along


def finish(net, value, rel, cuts, weights, gain, width, heads_from, into, so_far):
    half, cols = value.shape
    tile = BLOCK
    steps = half // tile
    widths = [sum(b - a for a, b in runs) for runs in cuts]
    narrow = widths[3] == BLOCK

    def body(place_ref, v_ref, wq_ref, wk_ref, wv_ref, gain_ref, *refs):
        outs = refs[-5:]
        v = v_ref[...].astype(F32)
        made = [jnp.concatenate([v[:, a:b] for a, b in runs], axis=1) for runs in cuts]
        for k, (out, m) in enumerate(zip(outs, made)):
            out[...] = m.T[:8] if k == 3 and narrow else m
        acc = made[0] * wq_ref[...].astype(F32)
        acc = acc + made[1] * wk_ref[...].astype(F32) + made[2] * wv_ref[...].astype(F32)
        part = jnp.broadcast_to(jnp.sum(acc, axis=1, keepdims=True), (tile, BLOCK)).T[:1]
        part = part / gain_ref[...]
        outs[4][...] = part if so_far is None else part + refs[0][...]

    def row(i, p):
        return (p[3] if rel == 0 else 1 - p[3]) * steps + i

    def cols_spec(w, at):
        return pl.BlockSpec((tile, w), lambda i, p: (row(i, p), at // w))

    def lanes_spec(rows):
        return pl.BlockSpec((rows, tile), lambda i, p: (0, row(i, p)))

    args = [value, *[far(w) for w in weights], gain.reshape(1, -1)]
    specs = [pl.BlockSpec((tile, cols), lambda i, p: (i, 0))]
    specs += [cols_spec(widths[0], heads_from)] * 3 + [lanes_spec(1)]
    alias = {}
    if so_far is not None:
        args.append(so_far)
        specs.append(lanes_spec(1))
    if into:
        alias = {1 + len(args) + k: k for k in range(len(into))}
        args += list(into)
        specs += [pl.BlockSpec(memory_space=pl.ANY)] * len(into)
    return pl.pallas_call(
        body,
        grid_spec=pltpu.PrefetchScalarGridSpec(
            num_scalar_prefetch=1,
            grid=(steps,),
            in_specs=specs,
            out_specs=[cols_spec(w, heads_from) for w in widths[:3]]
            + [lanes_spec(8) if narrow else cols_spec(widths[3], 0), lanes_spec(1)],
        ),
        out_shape=[pltpu.HBM((2 * half, width), F32)] * 3
        + [
            jax.ShapeDtypeStruct((8, 2 * half), F32) if narrow else pltpu.HBM((2 * half, width), F32),
            jax.ShapeDtypeStruct((1, 2 * half), F32),
        ],
        input_output_aliases=alias,
        compiler_params=pltpu.CompilerParams(vmem_limit_bytes=20 * 1024 * 1024),
        cost_estimate=brief,
        name="finish",
    )(net.places(), *args)


def project(tokens, gain, weights, groups):
    count, width = tokens.shape
    tile = min(256, count)
    pairs_here = width // BLOCK // groups

    def body(t_ref, gain_ref, *refs):
        out, nt_ref = refs[-2:]
        x = t_ref[...].astype(F32)
        inv = lax.rsqrt(jnp.mean(x * x, axis=1, keepdims=True) + epsilon)
        normed = x * inv * gain_ref[...]
        low = normed.astype(BF16)
        nt_ref[...] = normed.T.astype(BF16)
        for i, w in enumerate(refs[:-2]):
            r = dot(low, w[...]).astype(BF16)
            for p in range(groups * pairs_here):
                at = (3 * (p % pairs_here) + i) * BLOCK
                out[p // pairs_here, :, at : at + BLOCK] = r[:, BLOCK * p : BLOCK * p + BLOCK]

    return pl.pallas_call(
        body,
        grid=(count // tile,),
        in_specs=[
            pl.BlockSpec((tile, width), lambda i: (i, 0)),
            pl.BlockSpec((1, width), lambda i: (0, 0)),
        ]
        + [pl.BlockSpec((width, width), lambda i: (0, 0))] * 3,
        out_specs=[
            pl.BlockSpec((groups, tile, 3 * width // groups), lambda i: (0, i, 0)),
            pl.BlockSpec((width, tile), lambda i: (0, i)),
        ],
        out_shape=[
            pltpu.HBM((groups, count, 3 * width // groups), BF16),
            pltpu.HBM((width, count), BF16),
        ],
        compiler_params=pltpu.CompilerParams(vmem_limit_bytes=24 * 1024 * 1024),
        cost_estimate=brief,
        name="project",
    )(far(tokens), gain.reshape(1, -1), *[far(w) for w in weights])


def gelu_parts(pre):
    k0 = 0.7978845608028654
    k1 = 0.044715
    sq = pre * pre
    s = 0.5 * jnp.tanh(pre * (k0 + (k0 * k1) * sq)) + 0.5
    act = pre * s
    slope = s + (act - act * s) * (2.0 * k0 + (6.0 * k0 * k1) * sq)
    return act, slope


def before_ffn(mixed, w_out, tokens, gain, g):
    count, width = mixed.shape
    tile = min(256, count)

    def body(mixed_ref, w_ref, t_ref, gain_ref, g_ref, mid_ref, s_ref, st_ref, gt_ref):
        mid = t_ref[...].astype(F32) + dot(mixed_ref[...], w_ref[...])
        inv = lax.rsqrt(jnp.mean(mid * mid, axis=1, keepdims=True) + epsilon)
        second = mid * inv * gain_ref[...]
        mid_ref[...] = mid.astype(BF16)
        s_ref[...] = second.astype(BF16)
        st_ref[...] = second.T.astype(BF16)
        gt_ref[...] = g_ref[...].astype(F32).T.astype(BF16)

    def rows_of(w):
        return pl.BlockSpec((tile, w), lambda i: (i, 0))

    cols = pl.BlockSpec((width, tile), lambda i: (0, i))
    return pl.pallas_call(
        body,
        grid=(count // tile,),
        in_specs=[
            rows_of(width),
            pl.BlockSpec((width, width), lambda i: (0, 0)),
            rows_of(width),
            pl.BlockSpec((1, width), lambda i: (0, 0)),
            rows_of(width),
        ],
        out_specs=[rows_of(width), rows_of(width), cols, cols],
        out_shape=[
            pltpu.HBM((count, width), BF16),
            pltpu.HBM((count, width), BF16),
            pltpu.HBM((width, count), BF16),
            pltpu.HBM((width, count), BF16),
        ],
        compiler_params=pltpu.CompilerParams(vmem_limit_bytes=20 * 1024 * 1024),
        cost_estimate=brief,
        name="before_ffn",
    )(mixed, far(w_out), far(tokens), gain.reshape(1, -1), far(g))


def ffn(net, ups, downs, second, second_t, g, g_t, middle):
    nz, nx, hb, width = ups[0].shape
    count = g.shape[0]
    part = nx * hb
    tile = 256 if count % 256 == 0 else count
    lanes = 256 if width % 256 == 0 else width

    def body(
        place_ref, u0_ref, u1_ref, d0_ref, d1_ref, st_far, gt_far, g_far, s_far, m_far,
        out_ref, go_ref, gx_ref, gs_ref, act_ref, gu_ref, acc_ref, gsum_ref,
        st_ref, gt_ref, g_ref, s_ref, m_ref, sems,
    ):
        step = pl.program_id(0)
        st_copy, gt_copy, g_copy, s_copy, m_copy = [
            pltpu.make_async_copy(a, b, sems.at[i])
            for i, (a, b) in enumerate(
                (
                    (st_far, st_ref),
                    (gt_far, gt_ref),
                    (g_far, g_ref),
                    (s_far, s_ref),
                    (m_far, m_ref),
                )
            )
        ]

        @pl.when(step == 0)
        def _():
            for copy in (st_copy, gt_copy, g_copy, s_copy, m_copy):
                copy.start()
            st_copy.wait()
            gt_copy.wait()

        up_all, down_all = [
            jnp.concatenate([r[...].reshape(part, width) for r in refs], axis=0)
            for refs in ((u0_ref, u1_ref), (d0_ref, d1_ref))
        ]
        starts = list(range(0, count, tile))

        def both(t):
            return dot(up_all, st_ref[:, t : t + tile]), dot(down_all, gt_ref[:, t : t + tile])

        @pl.when(step == 0)
        def _():
            acc_ref[...] = jnp.zeros_like(acc_ref)
            gsum_ref[...] = jnp.zeros_like(gsum_ref)

        def sums(t):
            at = slice(t, t + tile)
            acc_ref[at] += dot(act_ref[:, at], down_all, CONTRACT_ROWS)
            gsum_ref[at] += dot(gu_ref[:, at], up_all, CONTRACT_ROWS)

        ahead = both(starts[0])
        for n, t in enumerate(starts):
            pre, gh = ahead
            if n + 1 < len(starts):
                ahead = both(starts[n + 1])
            act, slope = gelu_parts(pre)
            act_ref[:, t : t + tile] = act.astype(BF16)
            gu_ref[:, t : t + tile] = (gh * slope).astype(BF16)
            if n > 0:
                sums(starts[n - 1])
        sums(starts[-1])

        @pl.when(step == 0)
        def _():
            g_copy.wait()
            s_copy.wait()

        for k in range(0, width, lanes):
            cols = slice(k, k + lanes)
            gd = dot(act_ref[...], g_ref[:, cols]).astype(BF16)
            gu = dot(gu_ref[...], s_ref[:, cols]).astype(BF16)
            for rel in range(2):
                for i in range(nx):
                    at = part * rel + hb * i
                    out = (go_ref, gx_ref)[rel]
                    out[0, i, :, cols] = gd[at : at + hb]
                    out[1, i, :, cols] = gu[at : at + hb]

        @pl.when(step == nz - 1)
        def _():
            m_copy.wait()
            out_ref[...] = (m_ref[...].astype(F32) + acc_ref[...]).astype(BF16)
            gs_ref[...] = gsum_ref[...].astype(BF16)

    away = pl.BlockSpec(memory_space=pltpu.HBM)

    one = pl.BlockSpec((None, nx, hb, width), lambda i, p: (i, 0, 0, 0))
    two = pl.BlockSpec((None, 2, nx, hb, width), lambda i, p: (i, 0, 0, 0, 0))
    flat = pl.BlockSpec((count, width), lambda i, p: (0, 0))
    return pl.pallas_call(
        body,
        grid_spec=pltpu.PrefetchScalarGridSpec(
            num_scalar_prefetch=1,
            grid=(nz,),
            in_specs=[one] * 4 + [away] * 5,
            out_specs=[flat, two, two, flat],
            scratch_shapes=[
                pltpu.VMEM((2 * part, count), BF16),
                pltpu.VMEM((2 * part, count), BF16),
                pltpu.VMEM((count, width), F32),
                pltpu.VMEM((count, width), F32),
                pltpu.VMEM((width, count), BF16),
                pltpu.VMEM((width, count), BF16),
                pltpu.VMEM((count, width), BF16),
                pltpu.VMEM((count, width), BF16),
                pltpu.VMEM((count, width), BF16),
                pltpu.SemaphoreType.DMA((5,)),
            ],
        ),
        out_shape=[
            pltpu.HBM((count, width), BF16),
            pltpu.HBM((nz, 2, nx, hb, width), BF16),
            pltpu.HBM((nz, 2, nx, hb, width), BF16),
            pltpu.HBM((count, width), BF16),
        ],
        compiler_params=pltpu.CompilerParams(vmem_limit_bytes=42 * 1024 * 1024),
        cost_estimate=brief,
        name="ffn",
    )(net.places(), *ups, *downs, *[far(v) for v in (second_t, g_t, g, second, middle)])


def after_ffn(net, grad_second, middle, gain, g, w_out, mixed_t, cols):
    count, width = middle.shape
    half = width // 2
    tile = min(512, count)

    def body(
        place_ref, gs_ref, m_ref, gain_ref, g_ref, w_ref, mine_ref, theirs_ref,
        gm_ref, gx_ref, gg_ref, wo_ref, wx_ref, acc_ref,
    ):
        gs = gs_ref[...].astype(F32)
        m = m_ref[...].astype(F32)
        r = lax.rsqrt(jnp.mean(m * m, axis=1, keepdims=True) + epsilon)
        scaled = gs * gain_ref[...]
        mean = jnp.mean(scaled * m, axis=1, keepdims=True)
        gm = g_ref[...].astype(F32) + r * scaled - m * (r * r * r * mean)
        ga = gm.astype(BF16)
        gm_ref[...] = ga
        gx_ref[...] = dot(ga, w_ref[...], CONTRACT_LANES).astype(BF16)
        add = jnp.sum(gs * (m * r), axis=0, keepdims=True)
        step = pl.program_id(0)

        @pl.when(step == 0)
        def _():
            gg_ref[...] = add

        @pl.when(step != 0)
        def _():
            gg_ref[...] += add

        add_o = dot(jnp.concatenate([mine_ref[...], theirs_ref[...]], axis=0), ga)

        @pl.when(step == 0)
        def _():
            acc_ref[...] = add_o

        @pl.when(step != 0)
        def _():
            acc_ref[...] += add_o

        @pl.when(step == pl.num_programs(0) - 1)
        def _():
            wo_ref[...] = acc_ref[:half].astype(BF16)
            wx_ref[...] = acc_ref[half:].astype(BF16)

    def rows_of(w):
        return pl.BlockSpec((tile, w), lambda i, p: (i, 0))

    row = pl.BlockSpec((1, width), lambda i, p: (0, 0))
    grad = pl.BlockSpec((half, width), lambda i, p: (0, 0))
    return pl.pallas_call(
        body,
        grid_spec=pltpu.PrefetchScalarGridSpec(
            num_scalar_prefetch=1,
            grid=(count // tile,),
            in_specs=[
                rows_of(width),
                rows_of(width),
                row,
                rows_of(width),
                pl.BlockSpec((width, width), lambda i, p: (0, 0)),
                pl.BlockSpec((half, tile), lambda i, p: (p[3], i)),
                pl.BlockSpec((half, tile), lambda i, p: (1 - p[3], i)),
            ],
            out_specs=[rows_of(width), rows_of(width), row, grad, grad],
            scratch_shapes=[pltpu.VMEM((width, width), F32)],
        ),
        out_shape=[
            pltpu.HBM((count, width), BF16),
            jax.ShapeDtypeStruct((count, width), BF16),
            jax.ShapeDtypeStruct((1, width), F32),
            pltpu.HBM((half, cols), BF16),
            pltpu.HBM((half, cols), BF16),
        ],
        compiler_params=pltpu.CompilerParams(vmem_limit_bytes=24 * 1024 * 1024),
        cost_estimate=brief,
        name="after_ffn",
    )(net.places(), far(grad_second), far(middle), gain.reshape(1, -1), far(g), far(w_out), mixed_t, mixed_t)


def token_grad(dproj, weights, tokens, gain, grad_middle):
    count, width = tokens.shape
    tile = min(256, count)

    def body(*refs):
        d_refs = refs[: len(dproj)]
        w_refs = refs[len(dproj) : len(dproj) + 3]
        t_ref, gain_ref, gm_ref, out_ref = refs[len(dproj) + 3 :]
        gn = None
        for i, w in enumerate(w_refs):
            cols = []
            for d in d_refs:
                for p in range(d.shape[1] // (3 * BLOCK)):
                    at = (3 * p + i) * BLOCK
                    cols.append(d[:, at : at + BLOCK])
            r = dot(jnp.concatenate(cols, axis=1), w[...], CONTRACT_LANES)
            gn = r if gn is None else gn + r
        scaled = gn * gain_ref[...]
        x = t_ref[...].astype(F32)
        r = lax.rsqrt(jnp.mean(x * x, axis=1, keepdims=True) + epsilon)
        mean = jnp.mean(scaled * x, axis=1, keepdims=True)
        out_ref[...] = gm_ref[...].astype(F32) + r * scaled - x * (r * r * r * mean)

    def rows_of(w):
        return pl.BlockSpec((tile, w), lambda i: (i, 0))

    return pl.pallas_call(
        body,
        grid=(count // tile,),
        in_specs=[rows_of(d.shape[1]) for d in dproj]
        + [pl.BlockSpec(w.shape, lambda i: (0, 0)) for w in weights]
        + [rows_of(width), pl.BlockSpec((1, width), lambda i: (0, 0)), rows_of(width)],
        out_specs=rows_of(width),
        out_shape=pltpu.HBM((count, width), F32),
        compiler_params=pltpu.CompilerParams(vmem_limit_bytes=20 * 1024 * 1024),
        cost_estimate=brief,
        name="token_grad",
    )(*[far(d) for d in dproj], *[far(w) for w in weights], far(tokens), gain.reshape(1, -1), far(grad_middle))


def local(
    net,
    tokens,
    tasks,
    segments,
    buckets,
    w_query,
    w_key,
    w_value,
    w_out,
    w_up,
    w_down,
    bias_table,
    gain_attn,
    gain_ffn,
    cotangent,
):
    rows, length, width = tokens.shape
    groups, bucket_count, heads = bias_table.shape
    pairs = heads // 2
    count = rows * length
    parts = 3
    part = pairs // parts

    up_state = net.gather(w_up.T, "z")
    flat = tokens.reshape(count, width)
    proj, normed_t = project(flat, gain_attn, (w_query, w_key, w_value), parts)

    task_hot = (tasks[:, None] == jnp.arange(groups, dtype=jnp.int32)[None, :]).astype(F32)
    table_rows = jnp.einsum("rg,gbh->rbh", task_hot, bias_table, precision=highest)
    middle_offset = length - 1 + 3 * BLOCK
    near = buckets[middle_offset - WIDE + 1 : middle_offset + 1][::-1]
    bucket_hot = (near[None, :] == jnp.arange(bucket_count, dtype=jnp.int32)[:, None]).astype(F32)
    bias = jnp.einsum("rbh,bk->rhk", table_rows, bucket_hot, precision=highest)
    bias = bias.reshape(rows * pairs, 2, WIDE)
    seg = segments.reshape(count, 1)
    lane = jnp.arange(BLOCK, dtype=jnp.int32)[None, :]
    kseg = (lane == seg).astype(BF16)
    qseg = jnp.where((lane != seg) & (lane < 4), -1e30, 0.0).astype(BF16)

    def attend_part(first, pairs_here, proj, made):
        return attend(first, pairs_here, pairs, rows, length, proj, kseg, qseg, bias, made)

    up_state, (proj, w_down) = gather_1(net, up_state, (proj, w_down))
    down_state = net.gather(w_down, "z")
    made = attend_part(0, part, proj, None)
    up_state, (made, proj) = gather_2(net, up_state, (made, proj))
    made = attend_part(part, part, proj, made)
    down_state, (made, proj) = gather_1(net, down_state, (made, proj))
    made = attend_part(2 * part, pairs - 2 * part, proj, made)
    ups, made = gather_3(net, up_state, made)
    down_state, made = gather_2(net, down_state, made)
    mixed, mixed_t = made[2:]
    g = cotangent.reshape(count, width)
    middle, second, second_t, g_t = before_ffn(mixed, w_out, flat, gain_ffn, g)
    downs, second = gather_3(net, down_state, second)

    ups, downs, second = hold((ups, downs, second))
    output, gf_own, gf_other, grad_second = ffn(
        net, ups, downs, second, second_t, g, g_t, middle
    )
    gf_other, grad_second = hold((gf_other, grad_second))
    gf_theirs = net.fetch(gf_other, "c", 1)
    cols1 = width * parts
    cols2 = width + BLOCK
    cut1 = cols1 // 2
    cut2 = width // 2
    grad_middle, grad_mixed, grad_gain_ffn, *r1 = after_ffn(
        net, grad_second, middle, gain_ffn, g, w_out, mixed_t, cols1
    )
    sf, grad_mixed = scatter_1(net, gf_own, gf_theirs, grad_mixed)

    def back_part(i, grad_mixed, cols, buffers, at):
        d, off, *r = attend_grad(
            net, part * i, part, pairs, rows, length, proj, made, grad_mixed, normed_t, cols, buffers, at
        )
        return d, off, r

    dproj = [None] * parts
    doff = [None] * parts
    dproj[0], doff[0], r1 = back_part(0, grad_mixed, cols1, r1, width)
    dproj[1], doff[1], r1 = back_part(1, grad_mixed, cols1, r1, 2 * width)
    grad_mixed, r1, sf = hold((grad_mixed, r1, sf))
    r1_theirs = net.fetch(r1[1], "c", 1)
    state1, grad_mixed = reduce_1(net, r1[0], r1_theirs, cut1, grad_mixed, True)
    dproj[2], doff[2], r2 = back_part(2, grad_mixed, cols2, None, 0)
    state1, (doff, r2, dproj) = reduce_2(net, state1, (doff, r2, dproj), False)

    per_row = jnp.concatenate([d.reshape(part, rows, 2, WIDE) for d in doff], axis=0)
    per_row = per_row.transpose(1, 0, 2, 3).reshape(rows, heads, WIDE)
    grad_bucket = jnp.einsum("rhk,bk->rbh", per_row, bucket_hot, precision=highest)
    grad_table = jnp.einsum("rg,rbh->gbh", task_hot, grad_bucket, precision=highest)
    small = jnp.concatenate([grad_table.reshape(-1, width), grad_gain_ffn], axis=0)
    table_cols = small.shape[0] - 1
    small = jnp.pad(small.T, ((0, 0), (0, BLOCK - small.shape[0]))).astype(BF16)
    c = net.places()[3]
    half = width // 2
    r2 = [
        lax.dynamic_update_slice(
            r, lax.dynamic_slice_in_dim(small, at * half, half, axis=0), (0, width)
        )
        for r, at in zip(r2, (c, 1 - c))
    ]
    r2, dproj = hold((r2, dproj))
    r2_theirs = net.fetch(r2[1], "c", 1)
    grad_tokens = token_grad(
        dproj, (w_query, w_key, w_value), flat, gain_attn, grad_middle
    )
    state1, (r2, grad_tokens) = reduce_3(net, state1, (r2, grad_tokens))
    state2, grad_tokens = reduce_1(net, r2[0], r2_theirs, cut2, grad_tokens, False)
    state1, grad_tokens = fold_z(net, state1, grad_tokens)
    state2, grad_tokens = reduce_2(net, state2, grad_tokens, False)
    def head_runs(first, count_here, i):
        return [
            (first + (3 * p + i) * BLOCK, first + (3 * p + i + 1) * BLOCK)
            for p in range(count_here)
        ]

    front = pairs - (pairs - 2 * part)
    weights = (w_query, w_key, w_value)
    cuts1 = [head_runs(width, front, i) for i in range(3)] + [[(0, width)]]
    cuts2 = [head_runs(0, pairs - front, i) for i in range(3)] + [[(width, width + BLOCK)]]

    def finish_1(value, rel, into):
        return finish(net, value, rel, cuts1, weights, gain_attn, width, 0, into, None)

    def finish_2(value, rel, into):
        return finish(
            net, value, rel, cuts2, weights, gain_attn, width, front * BLOCK, into, made1[4]
        )

    state2, grad_tokens = reduce_3(net, state2, grad_tokens)
    last1, grad_tokens = spread_0(net, state1, grad_tokens)
    sf, grad_tokens = scatter_2(net, sf, grad_tokens)
    state2, grad_tokens = fold_z(net, state2, grad_tokens)
    last1, grad_tokens = spread_z(net, last1, grad_tokens)
    last2, grad_tokens = spread_0(net, state2, grad_tokens)
    last1, grad_tokens = spread_1(net, last1, cut1, grad_tokens)
    last2, grad_tokens = spread_z(net, last2, grad_tokens)
    sf, grad_tokens = scatter_3(net, sf, grad_tokens)
    last1, grad_tokens = spread_2(net, last1, grad_tokens)
    last2, grad_tokens = spread_1(net, last2, cut2, grad_tokens)
    sf, grad_tokens = fold_z(net, sf, grad_tokens)
    last1, grad_tokens = spread_3(net, last1, grad_tokens)
    made1 = finish_1(last1[0], 0, None)
    last2, (grad_tokens, made1) = spread_2(net, last2, (grad_tokens, made1))
    made1 = finish_1(last1[1], 1, made1)
    last2, (grad_tokens, sf, made1) = spread_3(net, last2, (grad_tokens, sf, made1))
    made2 = finish_2(last2[0], 0, made1[:3])
    grad_ffn = total(sf)
    grad_down, grad_up = grad_ffn[0], grad_ffn[1].T

    made2 = finish_2(last2[1], 1, made2)
    grad_query, grad_key, grad_value, small, gain_sum = made2
    grad_w_out = made1[3]
    grad_table = small[:table_cols].reshape(groups, bucket_count, heads)
    return (
        output.reshape(rows, length, width),
        grad_tokens.reshape(rows, length, width),
        grad_query,
        grad_key,
        grad_value,
        grad_w_out,
        grad_up,
        grad_down,
        grad_table,
        gain_sum.reshape(-1),
        small[table_cols],
    )


def solution(mesh):
    in_specs = (
        P(("ma", "an"), None, None),
        P(("ma", "an")),
        P(("ma", "an"), None),
        P(),
        P(),
        P(),
        P(),
        P(),
        P("ma", "an"),
        P("an", "ma"),
        P(),
        P(),
        P(),
        P(("ma", "an"), None, None),
    )
    out_specs = (
        P(("ma", "an"), None, None),
        P(("ma", "an"), None, None),
        P(),
        P(),
        P(),
        P(),
        P("ma", "an"),
        P("an", "ma"),
        P(),
        P(),
        P(),
    )

    def whole(*args):
        net = Links(mesh.shape["ma"], mesh.shape["an"], args[0].shape[-1])
        return local(net, *args)

    return jax.shard_map(whole, mesh=mesh, in_specs=in_specs, out_specs=out_specs, check_vma=False)
```

profile of v0, /device:TPU:0, one launch (start us, length us, event | category | flops | bytes accessed | tf_op | source)
XLA Modules:
  0.0 282.8 jit_solution(11925032892379034645)
XLA Ops:
  0.7 3.1 %collective-permute-start = (bf16[192,384]{1,0:T(8,128)(2,1)}, bf16[192,384]{1,0:T(8,128)(2,1)S(1)}, u32[]{:S(2)}, u32[]{:S(2)}) collective-permute-start(bf16[192,384]{1,0:T(8,128)(2,1)} %bitcast.38), channel_id=1, source_target_pairs={{0,4},{1,5},{2,6},{3,7},{4,8},{5,9},{6,10},{7,11},{8,12},{9,13},{1... | collective-permute-start | bytes 442376 | tf_op jit(solution)/shard_map/ppermute | solution.py:377
  3.7 2.6 collective-permute-start.1
  11.1 8.2 %project.1 = (bf16[3,1024,768]{2,1,0:T(8,128)(2,1)}, bf16[768,1024]{1,0:T(8,128)(2,1)}) custom-call(bf16[1024,768]{1,0:T(8,128)(2,1)} %bitcast.48, f32[1,768]{1,0:T(1,128)S(1)} %reshape.81.gain_ref.refs_7_, bf16[768,768]{1,0:T(8,128)(2,1)} %wq_ref.7, bf16[768,768]{1,0:T(8,128)(2,1)} %wk_ref.7, bf16[768,768]{1,0:T(8,128)(2,1)} %wv_ref.7), custom_call_target="tpu_custom_call" | custom-call | flops 1000 | bytes 1000 | tf_op jit(solution)/shard_map/project/pallas_call | solution.py:706
  23.4 7.1 %attend.3 = (bf16[12,2,512,512]{3,2,1,0:T(8,128)(2,1)}, f32[12,2,512]{2,1,0:T(2,128)S(1)}, bf16[1024,768]{1,0:T(8,128)(2,1)S(1)}, bf16[768,1024]{1,0:T(8,128)(2,1)S(1)}) custom-call(bf16[3,1024,768]{2,1,0:T(8,128)(2,1)} %get-tuple-element.465.p_ref, bf16[1024,128]{1,0:T(8,128)(2,1)S(1)} %fusion.kseg_ref, bf16[1024,128]{1,0:T(8,128)(2,1)S(1)} %select_convert_fusion.qseg_ref, ...), custom_call_target="tpu_custom_call" | custom-call | flops 1000 | bytes 1000 | tf_op jit(solution)/shard_map/attend/pallas_call | solution.py:125
  36.1 7.0 %attend.4 = (bf16[12,2,512,512]{3,2,1,0:T(8,128)(2,1)}, f32[12,2,512]{2,1,0:T(2,128)S(1)}, bf16[1024,768]{1,0:T(8,128)(2,1)S(1)}, bf16[768,1024]{1,0:T(8,128)(2,1)S(1)}) custom-call(bf16[3,1024,768]{2,1,0:T(8,128)(2,1)} %get-tuple-element.465.p_ref, ...), custom_call_target="tpu_custom_call", output_to_operand_aliasing={{0}: (4, {}), {1}: (5, {}), {2}: (6, {}), {3}: (7, {})} | custom-call | flops 1000 | bytes 1000 | tf_op jit(solution)/shard_map/attend/pallas_call | solution.py:125
  47.9 7.0 %attend.5 = (bf16[12,2,512,512]{3,2,1,0:T(8,128)(2,1)}, f32[12,2,512]{2,1,0:T(2,128)S(1)}, bf16[1024,768]{1,0:T(8,128)(2,1)S(1)}, bf16[768,1024]{1,0:T(8,128)(2,1)S(1)}) custom-call(bf16[3,1024,768]{2,1,0:T(8,128)(2,1)} %get-tuple-element.465.p_ref, ...), custom_call_target="tpu_custom_call", output_to_operand_aliasing={{0}: (4, {}), {1}: (5, {}), {2}: (6, {}), {3}: (7, {})} | custom-call | flops 1000 | bytes 1000 | tf_op jit(solution)/shard_map/attend/pallas_call | solution.py:125
  57.7 6.5 %before_ffn.1 = (bf16[1024,768]{1,0:T(8,128)(2,1)}, bf16[1024,768]{1,0:T(8,128)(2,1)}, bf16[768,1024]{1,0:T(8,128)(2,1)}, bf16[768,1024]{1,0:T(8,128)(2,1)}) custom-call(bf16[1024,768]{1,0:T(8,128)(2,1)S(1)} %get-tuple-element.501.mixed_ref.o_ref, bf16[768,768]{1,0:T(8,128)(2,1)} %w_ref.3, bf16[1024,768]{1,0:T(8,128)(2,1)} %bitcast.49, ...), custom_call_target="tpu_custom_call" | custom-call | flops 1000 | bytes 1000 | tf_op jit(solution)/shard_map/before_ffn/pallas_call | solution.py:755
  64.3 6.8 %collective-permute-done.13.refs_1_ = bf16[4,2,96,384]{3,2,1,0:T(8,128)(2,1)S(1)} collective-permute-done((bf16[4,2,96,384]{3,2,1,0:T(8,128)(2,1)S(1)}, bf16[4,2,96,384]{3,2,1,0:T(8,128)(2,1)S(1)}, u32[]{:S(2)}, u32[]{:S(2)}) %collective-permute-start.13) | collective-permute-done | bytes 589856 | tf_op jit(solution)/shard_map/ppermute | solution.py:371
  72.2 4.5 %collective-permute-done.15.d1_ref = bf16[4,2,192,768]{3,2,1,0:T(8,128)(2,1)S(1)} collective-permute-done((bf16[4,2,192,768]{3,2,1,0:T(8,128)(2,1)S(1)}, bf16[4,2,192,768]{3,2,1,0:T(8,128)(2,1)S(1)}, u32[]{:S(2)}, u32[]{:S(2)}) %collective-permute-start.15) | collective-permute-done | bytes 2359328 | tf_op jit(solution)/shard_map/ppermute | solution.py:377
  76.7 39.1 %ffn.1 = (bf16[1024,768]{1,0:T(8,128)(2,1)}, bf16[4,2,2,192,768]{4,3,2,1,0:T(8,128)(2,1)}, bf16[4,2,2,192,768]{4,3,2,1,0:T(8,128)(2,1)}, bf16[1024,768]{1,0:T(8,128)(2,1)}) custom-call(s32[4]{0:T(128)S(1)} %pad_add_fusion.place_ref, bf16[4,2,192,768]{3,2,1,0:T(8,128)(2,1)S(1)} %gather_yx.2.u0_ref, ...), custom_call_target="tpu_custom_call" | custom-call | flops 1000 | bytes 1000 | tf_op jit(solution)/shard_map/ffn/pallas_call | solution.py:869
  116.0 10.0 %after_ffn.1 = (bf16[1024,768]{1,0:T(8,128)(2,1)}, bf16[1024,768]{1,0:T(8,128)(2,1)S(1)}, f32[1,768]{1,0:T(1,128)S(1)}, bf16[384,2304]{1,0:T(8,128)(2,1)}, bf16[384,2304]{1,0:T(8,128)(2,1)}) custom-call(s32[4]{0:T(128)S(1)} %pad_add_fusion.place_ref, bf16[1024,768]{1,0:T(8,128)(2,1)} %get-tuple-element.523.gs_ref, ...), custom_call_target="tpu_custom_call" | custom-call | flops 1000 | bytes 1000 | tf_op jit(solution)/shard_map/after_ffn/pallas_call | solution.py:950
  126.1 2.1 scatter_yx.1
  130.4 11.8 %attend_grad.3 = (bf16[1024,768]{1,0:T(8,128)(2,1)}, f32[4,2,768]{2,1,0:T(2,128)S(1)}, bf16[384,2304]{1,0:T(8,128)(2,1)}, bf16[384,2304]{1,0:T(8,128)(2,1)}) custom-call(s32[4]{0:T(128)S(1)} %pad_add_fusion.place_ref, bf16[3,1024,768]{2,1,0:T(8,128)(2,1)} %get-tuple-element.465.p_ref, ...), custom_call_target="tpu_custom_call", output_to_operand_aliasing={{2}: (8, {}), {3}: (9, {})} | custom-call | flops 1000 | bytes 1000 | tf_op jit(solution)/shard_map/attend_grad/pallas_call | solution.py:286
  142.3 11.9 %attend_grad.4 = (bf16[1024,768]{1,0:T(8,128)(2,1)}, f32[4,2,768]{2,1,0:T(2,128)S(1)}, bf16[384,2304]{1,0:T(8,128)(2,1)}, bf16[384,2304]{1,0:T(8,128)(2,1)}) custom-call(s32[4]{0:T(128)S(1)} %pad_add_fusion.place_ref, bf16[3,1024,768]{2,1,0:T(8,128)(2,1)} %get-tuple-element.465.p_ref, ...), custom_call_target="tpu_custom_call", output_to_operand_aliasing={{2}: (8, {}), {3}: (9, {})} | custom-call | flops 1000 | bytes 1000 | tf_op jit(solution)/shard_map/attend_grad/pallas_call | solution.py:286
  154.2 2.1 collective-permute-done.17.refs_1_
  157.6 3.9 %collective-permute-done.19.refs_1_ = bf16[384,2304]{1,0:T(8,128)(2,1)S(1)} collective-permute-done((bf16[384,2304]{1,0:T(8,128)(2,1)}, bf16[384,2304]{1,0:T(8,128)(2,1)S(1)}, u32[]{:S(2)}, u32[]{:S(2)}) %collective-permute-start.19) | collective-permute-done | bytes 1769504 | tf_op jit(solution)/shard_map/ppermute | solution.py:377
  163.0 2.0 reduce_yx.2
  166.0 11.9 %attend_grad.5 = (bf16[1024,768]{1,0:T(8,128)(2,1)}, f32[4,2,768]{2,1,0:T(2,128)S(1)}, bf16[384,896]{1,0:T(8,128)(2,1)}, bf16[384,896]{1,0:T(8,128)(2,1)}) custom-call(s32[4]{0:T(128)S(1)} %pad_add_fusion.place_ref, bf16[3,1024,768]{2,1,0:T(8,128)(2,1)} %get-tuple-element.465.p_ref, bf16[12,2,512,512]{3,2,1,0:T(8,128)(2,1)} %get-tuple-element.534.u_ref, ...), custom_call_target="tpu_custom_call" | custom-call | flops 1000 | bytes 1000 | tf_op jit(solution)/shard_map/attend_grad/pallas_call | solution.py:286
  177.9 2.0 reduce_xy.2
  184.3 9.6 %token_grad.1 = f32[1024,768]{1,0:T(8,128)} custom-call(bf16[1024,768]{1,0:T(8,128)(2,1)} %get-tuple-element.601.refs_0_, bf16[1024,768]{1,0:T(8,128)(2,1)} %get-tuple-element.602.refs_1_, bf16[1024,768]{1,0:T(8,128)(2,1)} %get-tuple-element.603.refs_2_, bf16[768,768]{1,0:T(8,128)(2,1)} %wq_ref.7, bf16[768,768]{1,0:T(8,128)(2,1)} %wk_ref.7, ...), custom_call_target="tpu_custom_call" | custom-call | flops 1000 | bytes 1000 | tf_op jit(solution)/shard_map/token_grad/pallas_call | solution.py:1006
  194.7 3.8 %collective-permute-start.27 = (bf16[2,24,2304]{2,1,0:T(8,128)(2,1)S(1)}, bf16[2,24,2304]{2,1,0:T(8,128)(2,1)S(1)}, u32[]{:S(2)}, u32[]{:S(2)}) collective-permute-start(bf16[2,24,2304]{2,1,0:T(8,128)(2,1)S(1)} %get-tuple-element.627), channel_id=1, source_target_pairs={{0,4},{1,5},{2,6},{3,7},{4,0},{5,1},{6,2},{7,3},{8,12},{9,13},{10,... | collective-permute-start | bytes 663560 | tf_op jit(solution)/shard_map/ppermute | solution.py:385
  200.4 3.5 %collective-permute-done.27.refs_1_ = bf16[2,24,2304]{2,1,0:T(8,128)(2,1)S(1)} collective-permute-done((bf16[2,24,2304]{2,1,0:T(8,128)(2,1)S(1)}, bf16[2,24,2304]{2,1,0:T(8,128)(2,1)S(1)}, u32[]{:S(2)}, u32[]{:S(2)}) %collective-permute-start.27) | collective-permute-done | bytes 221216 | tf_op jit(solution)/shard_map/ppermute | solution.py:385
  207.9 3.7 %collective-permute-done.28.refs_1_ = bf16[96,384]{1,0:T(8,128)(2,1)S(1)} collective-permute-done((bf16[96,384]{1,0:T(8,128)(2,1)S(1)}, bf16[96,384]{1,0:T(8,128)(2,1)S(1)}, u32[]{:S(2)}, u32[]{:S(2)}) %collective-permute-start.28) | collective-permute-done | bytes 73760 | tf_op jit(solution)/shard_map/ppermute | solution.py:377
  219.6 4.3 %collective-permute-done.30.refs_1_ = bf16[2,24,896]{2,1,0:T(8,128)(2,1)S(1)} collective-permute-done((bf16[2,24,896]{2,1,0:T(8,128)(2,1)S(1)}, bf16[2,24,896]{2,1,0:T(8,128)(2,1)S(1)}, u32[]{:S(2)}, u32[]{:S(2)}) %collective-permute-start.30) | collective-permute-done | bytes 86048 | tf_op jit(solution)/shard_map/ppermute | solution.py:385
  226.9 3.8 %collective-permute-done.32.refs_1_ = bf16[24,896]{1,0:T(8,128)(2,1)S(1)} collective-permute-done((bf16[24,896]{1,0:T(8,128)(2,1)S(1)}, bf16[24,896]{1,0:T(8,128)(2,1)S(1)}, u32[]{:S(2)}, u32[]{:S(2)}) %collective-permute-start.32) | collective-permute-done | bytes 43040 | tf_op jit(solution)/shard_map/ppermute | solution.py:385
  236.2 3.1 %collective-permute-done.34.refs_1_ = bf16[24,896]{1,0:T(8,128)(2,1)S(1)} collective-permute-done((bf16[24,896]{1,0:T(8,128)(2,1)S(1)}, bf16[24,896]{1,0:T(8,128)(2,1)S(1)}, u32[]{:S(2)}, u32[]{:S(2)}) %collective-permute-start.34) | collective-permute-done | bytes 43040 | tf_op jit(solution)/shard_map/ppermute | solution.py:385
  245.9 6.4 %collective-permute-done.36.refs_1_ = bf16[2,24,896]{2,1,0:T(8,128)(2,1)S(1)} collective-permute-done((bf16[2,24,896]{2,1,0:T(8,128)(2,1)S(1)}, bf16[2,24,896]{2,1,0:T(8,128)(2,1)S(1)}, u32[]{:S(2)}, u32[]{:S(2)}) %collective-permute-start.36) | collective-permute-done | bytes 86048 | tf_op jit(solution)/shard_map/ppermute | solution.py:385
  255.8 2.4 collective-permute-start.48
  258.6 4.4 %finish.4 = (f32[768,768]{1,0:T(8,128)}, f32[768,768]{1,0:T(8,128)}, f32[768,768]{1,0:T(8,128)}, f32[768,768]{1,0:T(8,128)}, f32[1,768]{1,0:T(1,128)S(1)}) custom-call(s32[4]{0:T(128)S(1)} %pad_add_fusion.place_ref, bf16[384,2304]{1,0:T(8,128)(2,1)S(1)} %spread_yx.2.v_ref, bf16[768,768]{1,0:T(8,128)(2,1)} %wq_ref.7, bf16[768,768]{1,0:T(8,128)(2,1)} %wk_ref.7, ...), custom_call_target="tpu_custom_call" | custom-call | flops 1000 | bytes 1000 | tf_op jit(solution)/shard_map/finish/pallas_call | solution.py:667
  265.7 4.4 %finish.5 = (f32[768,768]{1,0:T(8,128)}, f32[768,768]{1,0:T(8,128)}, f32[768,768]{1,0:T(8,128)}, f32[768,768]{1,0:T(8,128)}, f32[1,768]{1,0:T(1,128)S(1)}) custom-call(s32[4]{0:T(128)S(1)} %pad_add_fusion.place_ref, ...), custom_call_target="tpu_custom_call", output_to_operand_aliasing={{0}: (6, {}), {1}: (7, {}), {2}: (8, {}), {3}: (9, {}), {4}... | custom-call | flops 1000 | bytes 1000 | tf_op jit(solution)/shard_map/finish/pallas_call | solution.py:667
  272.8 3.5 %finish.6 = (f32[768,768]{1,0:T(8,128)}, f32[768,768]{1,0:T(8,128)}, f32[768,768]{1,0:T(8,128)}, f32[8,768]{1,0:T(8,128)S(1)}, f32[1,768]{1,0:T(1,128)S(1)}) custom-call(s32[4]{0:T(128)S(1)} %pad_add_fusion.place_ref, bf16[384,896]{1,0:T(8,128)(2,1)S(1)} %spread_yx.3.v_ref, ...), custom_call_target="tpu_custom_call", output_to_operand_aliasing={{0}: (7, {}), {1}: (8, {}), {2}: (9, {})} | custom-call | flops 1000 | bytes 1000 | tf_op jit(solution)/shard_map/finish/pallas_call | solution.py:667
  277.2 3.5 %finish.7 = (f32[768,768]{1,0:T(8,128)}, f32[768,768]{1,0:T(8,128)}, f32[768,768]{1,0:T(8,128)}, f32[8,768]{1,0:T(8,128)S(1)}, f32[1,768]{1,0:T(1,128)S(1)}) custom-call(s32[4]{0:T(128)S(1)} %pad_add_fusion.place_ref, ...), custom_call_target="tpu_custom_call", output_to_operand_aliasing={{0}: (7, {}), {1}: (8, {}), {2}: (9, {}), {3}: (10, {}), {4... | custom-call | flops 1000 | bytes 1000 | tf_op jit(solution)/shard_map/finish/pallas_call | solution.py:667
  (187 shorter events, 75.6 us)
Async XLA Ops:
  0.7 18.8 %collective-permute-start = (bf16[192,384]{1,0:T(8,128)(2,1)}, bf16[192,384]{1,0:T(8,128)(2,1)S(1)}, u32[]{:S(2)}, u32[]{:S(2)}) collective-permute-start(bf16[192,384]{1,0:T(8,128)(2,1)} %bitcast.38), channel_id=1, source_target_pairs={{0,4},{1,5},{2,6},{3,7},{4,8},{5,9},{6,10},{7,11},{8,12},{9,13},{1... | collective-permute-start | bytes 442376 | tf_op jit(solution)/shard_map/ppermute | solution.py:377
  3.7 15.7 %collective-permute-start.1 = (bf16[192,384]{1,0:T(8,128)(2,1)}, bf16[192,384]{1,0:T(8,128)(2,1)S(1)}, u32[]{:S(2)}, u32[]{:S(2)}) collective-permute-start(bf16[192,384]{1,0:T(8,128)(2,1)} %bitcast.39), channel_id=1, source_target_pairs={{0,8},{1,9},{2,10},{3,11},{4,12},{5,13},{6,14},{7,15},{8,0},{9,1},... | collective-permute-start | bytes 442376 | tf_op jit(solution)/shard_map/ppermute | solution.py:377
  6.3 13.1 %collective-permute-start.2 = (bf16[192,384]{1,0:T(8,128)(2,1)}, bf16[192,384]{1,0:T(8,128)(2,1)S(1)}, u32[]{:S(2)}, u32[]{:S(2)}) collective-permute-start(bf16[192,384]{1,0:T(8,128)(2,1)} %bitcast.40), channel_id=1, source_target_pairs={{0,12},{1,13},{2,14},{3,15},{4,0},{5,1},{6,2},{7,3},{8,4},{9,5},{1... | collective-permute-start | bytes 442376 | tf_op jit(solution)/shard_map/ppermute | solution.py:377
  20.1 10.4 %collective-permute-start.3 = (bf16[4,96,384]{2,1,0:T(8,128)(2,1)S(1)}, bf16[4,96,384]{2,1,0:T(8,128)(2,1)S(1)}, u32[]{:S(2)}, u32[]{:S(2)}) collective-permute-start(bf16[4,96,384]{2,1,0:T(8,128)(2,1)S(1)} %get-tuple-element.431.refs_0_), channel_id=1, source_target_pairs={{0,2},{1,3},{2,0},{3,1},{4,6},{5,7},{6,4},{7,5},{8,10},{9,11},{10,... | collective-permute-start | bytes 884744 | tf_op jit(solution)/shard_map/ppermute | solution.py:377
  31.2 23.7 %collective-permute-start.5 = (bf16[4,2,96,384]{3,2,1,0:T(8,128)(2,1)S(1)}, bf16[4,2,96,384]{3,2,1,0:T(8,128)(2,1)S(1)}, u32[]{:S(2)}, u32[]{:S(2)}) collective-permute-start(bf16[4,2,96,384]{3,2,1,0:T(8,128)(2,1)S(1)} %get-tuple-element.474.refs_0_), channel_id=1, source_target_pairs={{0,16},{16,0},{1,17},{17,1},{2,18},{18,2},{3,19},{19,3},{4,20},{20... | collective-permute-start | bytes 1769480 | tf_op jit(solution)/shard_map/ppermute | solution.py:371
  31.8 23.2 %collective-permute-start.6 = (bf16[4,96,768]{2,1,0:T(8,128)(2,1)S(1)}, bf16[4,96,768]{2,1,0:T(8,128)(2,1)S(1)}, u32[]{:S(2)}, u32[]{:S(2)}) collective-permute-start(bf16[4,96,768]{2,1,0:T(8,128)(2,1)S(1)} %get-tuple-element.476.refs_2_), channel_id=1, source_target_pairs={{0,2},{1,3},{2,0},{3,1},{4,6},{5,7},{6,4},{7,5},{8,10},{9,11},{10,... | collective-permute-start | bytes 1769480 | tf_op jit(solution)/shard_map/ppermute | solution.py:377
  32.3 10.8 %collective-permute-start.7 = (bf16[192,384]{1,0:T(8,128)(2,1)S(1)}, bf16[192,384]{1,0:T(8,128)(2,1)S(1)}, u32[]{:S(2)}, u32[]{:S(2)}) collective-permute-start(bf16[192,384]{1,0:T(8,128)(2,1)S(1)} %copy-done.15), channel_id=1, source_target_pairs={{0,4},{1,5},{2,6},{3,7},{4,8},{5,9},{6,10},{7,11},{8,12},{9,13},{1... | collective-permute-start | bytes 442376 | tf_op jit(solution)/shard_map/ppermute | solution.py:377
  33.5 10.7 %collective-permute-start.8 = (bf16[192,384]{1,0:T(8,128)(2,1)S(1)}, bf16[192,384]{1,0:T(8,128)(2,1)S(1)}, u32[]{:S(2)}, u32[]{:S(2)}) collective-permute-start(bf16[192,384]{1,0:T(8,128)(2,1)S(1)} %copy-done.15), channel_id=1, source_target_pairs={{0,8},{1,9},{2,10},{3,11},{4,12},{5,13},{6,14},{7,15},{8,0},{9,1},... | collective-permute-start | bytes 442376 | tf_op jit(solution)/shard_map/ppermute | solution.py:377
  34.3 9.9 %collective-permute-start.9 = (bf16[192,384]{1,0:T(8,128)(2,1)S(1)}, bf16[192,384]{1,0:T(8,128)(2,1)S(1)}, u32[]{:S(2)}, u32[]{:S(2)}) collective-permute-start(bf16[192,384]{1,0:T(8,128)(2,1)S(1)} %copy-done.15), channel_id=1, source_target_pairs={{0,12},{1,13},{2,14},{3,15},{4,0},{5,1},{6,2},{7,3},{8,4},{9,5},{1... | collective-permute-start | bytes 442376 | tf_op jit(solution)/shard_map/ppermute | solution.py:377
  44.9 10.9 %collective-permute-start.11 = (bf16[4,96,384]{2,1,0:T(8,128)(2,1)S(1)}, bf16[4,96,384]{2,1,0:T(8,128)(2,1)S(1)}, u32[]{:S(2)}, u32[]{:S(2)}) collective-permute-start(bf16[4,96,384]{2,1,0:T(8,128)(2,1)S(1)} %get-tuple-element.489.refs_0_), channel_id=1, source_target_pairs={{0,2},{1,3},{2,0},{3,1},{4,6},{5,7},{6,4},{7,5},{8,10},{9,11},{10,... | collective-permute-start | bytes 884744 | tf_op jit(solution)/shard_map/ppermute | solution.py:377
  46.4 9.3 %collective-permute-start.12 = (bf16[4,96,384]{2,1,0:T(8,128)(2,1)S(1)}, bf16[4,96,384]{2,1,0:T(8,128)(2,1)S(1)}, u32[]{:S(2)}, u32[]{:S(2)}) collective-permute-start(bf16[4,96,384]{2,1,0:T(8,128)(2,1)S(1)} %get-tuple-element.491.refs_2_), channel_id=1, source_target_pairs={{0,16},{16,0},{1,17},{17,1},{2,18},{18,2},{3,19},{19,3},{4,20},{20... | collective-permute-start | bytes 884744 | tf_op jit(solution)/shard_map/ppermute | solution.py:371
  56.5 14.6 %collective-permute-start.13 = (bf16[4,2,96,384]{3,2,1,0:T(8,128)(2,1)S(1)}, bf16[4,2,96,384]{3,2,1,0:T(8,128)(2,1)S(1)}, u32[]{:S(2)}, u32[]{:S(2)}) collective-permute-start(bf16[4,2,96,384]{3,2,1,0:T(8,128)(2,1)S(1)} %get-tuple-element.503.refs_0_), channel_id=1, source_target_pairs={{0,16},{16,0},{1,17},{17,1},{2,18},{18,2},{3,19},{19,3},{4,20},{20... | collective-permute-start | bytes 1769480 | tf_op jit(solution)/shard_map/ppermute | solution.py:371
  57.2 14.1 %collective-permute-start.14 = (bf16[4,96,768]{2,1,0:T(8,128)(2,1)S(1)}, bf16[4,96,768]{2,1,0:T(8,128)(2,1)S(1)}, u32[]{:S(2)}, u32[]{:S(2)}) collective-permute-start(bf16[4,96,768]{2,1,0:T(8,128)(2,1)S(1)} %get-tuple-element.505.refs_2_), channel_id=1, source_target_pairs={{0,2},{1,3},{2,0},{3,1},{4,6},{5,7},{6,4},{7,5},{8,10},{9,11},{10,... | collective-permute-start | bytes 1769480 | tf_op jit(solution)/shard_map/ppermute | solution.py:377
  57.7 14.5 %collective-permute-start.10 = (bf16[4,2,192,768]{3,2,1,0:T(8,128)(2,1)S(1)}, bf16[4,2,192,768]{3,2,1,0:T(8,128)(2,1)S(1)}, u32[]{:S(2)}, u32[]{:S(2)}) collective-permute-start(bf16[4,2,192,768]{3,2,1,0:T(8,128)(2,1)S(1)} %gather_yx.2.u0_ref), channel_id=1, source_target_pairs={{0,1},{1,0},{2,3},{3,2},{4,5},{5,4},{6,7},{7,6},{8,9},{9,8},{10,11... | collective-permute-start | bytes 7077896 | tf_op jit(solution)/shard_map/ppermute | solution.py:377
  115.8 10.2 %collective-permute-start.16 = (bf16[4,2,2,192,768]{4,3,2,1,0:T(8,128)(2,1)}, bf16[4,2,2,192,768]{4,3,2,1,0:T(8,128)(2,1)S(1)}, u32[]{:S(2)}, u32[]{:S(2)}) collective-permute-start(bf16[4,2,2,192,768]{4,3,2,1,0:T(8,128)(2,1)} %get-tuple-element.522), channel_id=1, source_target_pairs={{0,1},{1,0},{2,3},{3,2},{4,5},{5,4},{6,7},{7,6},{8,9},{9,8},{10,11... | collective-permute-start | bytes 14155784 | tf_op jit(solution)/shard_map/ppermute | solution.py:377
  128.2 28.1 %collective-permute-start.17 = (bf16[4,2,2,96,384]{4,3,2,1,0:T(8,128)(2,1)S(1)}, bf16[4,2,2,96,384]{4,3,2,1,0:T(8,128)(2,1)S(1)}, u32[]{:S(2)}, u32[]{:S(2)}) collective-permute-start(bf16[4,2,2,96,384]{4,3,2,1,0:T(8,128)(2,1)S(1)} %get-tuple-element.544), channel_id=1, source_target_pairs={{0,16},{16,0},{1,17},{17,1},{2,18},{18,2},{3,19},{19,3},{4,20},{20... | collective-permute-start | bytes 3538952 | tf_op jit(solution)/shard_map/ppermute | solution.py:371
  129.9 27.7 %collective-permute-start.18 = (bf16[4,2,96,768]{3,2,1,0:T(8,128)(2,1)S(1)}, bf16[4,2,96,768]{3,2,1,0:T(8,128)(2,1)S(1)}, u32[]{:S(2)}, u32[]{:S(2)}) collective-permute-start(bf16[4,2,96,768]{3,2,1,0:T(8,128)(2,1)S(1)} %get-tuple-element.546), channel_id=1, source_target_pairs={{0,2},{1,3},{2,0},{3,1},{4,6},{5,7},{6,4},{7,5},{8,10},{9,11},{10,... | collective-permute-start | bytes 3538952 | tf_op jit(solution)/shard_map/ppermute | solution.py:377
  165.0 12.9 %collective-permute-start.20 = (bf16[192,1152]{1,0:T(8,128)(2,1)}, bf16[192,1152]{1,0:T(8,128)(2,1)}, u32[]{:S(2)}, u32[]{:S(2)}) collective-permute-start(bf16[192,1152]{1,0:T(8,128)(2,1)} %get-tuple-element.558), channel_id=1, source_target_pairs={{0,16},{16,0},{1,17},{17,1},{2,18},{18,2},{3,19},{19,3},{4,20},{20... | collective-permute-start | bytes 1327112 | tf_op jit(solution)/shard_map/ppermute | solution.py:371
  165.4 12.5 %collective-permute-start.21 = (bf16[192,1152]{1,0:T(8,128)(2,1)}, bf16[192,1152]{1,0:T(8,128)(2,1)}, u32[]{:S(2)}, u32[]{:S(2)}) collective-permute-start(bf16[192,1152]{1,0:T(8,128)(2,1)} %get-tuple-element.560), channel_id=1, source_target_pairs={{0,2},{1,3},{2,0},{3,1},{4,6},{5,7},{6,4},{7,5},{8,10},{9,11},{10,... | collective-permute-start | bytes 1327112 | tf_op jit(solution)/shard_map/ppermute | solution.py:377
  181.1 17.4 %collective-permute-start.24 = (bf16[384,896]{1,0:T(8,128)(2,1)S(1)}, bf16[384,896]{1,0:T(8,128)(2,1)S(1)}, u32[]{:S(2)}, u32[]{:S(2)}) collective-permute-start(bf16[384,896]{1,0:T(8,128)(2,1)S(1)} %get-tuple-element.600), channel_id=1, source_target_pairs={{0,1},{1,0},{2,3},{3,2},{4,5},{5,4},{6,7},{7,6},{8,9},{9,8},{10,11... | collective-permute-start | bytes 2064392 | tf_op jit(solution)/shard_map/ppermute | solution.py:377
  181.2 12.7 %collective-permute-start.22 = (bf16[96,1152]{1,0:T(8,128)(2,1)S(1)}, bf16[96,1152]{1,0:T(8,128)(2,1)S(1)}, u32[]{:S(2)}, u32[]{:S(2)}) collective-permute-start(bf16[96,1152]{1,0:T(8,128)(2,1)S(1)} %get-tuple-element.587), channel_id=1, source_target_pairs={{0,2},{1,3},{2,0},{3,1},{4,6},{5,7},{6,4},{7,5},{8,10},{9,11},{10,... | collective-permute-start | bytes 663560 | tf_op jit(solution)/shard_map/ppermute | solution.py:377
  182.7 11.2 %collective-permute-start.23 = (bf16[96,1152]{1,0:T(8,128)(2,1)S(1)}, bf16[96,1152]{1,0:T(8,128)(2,1)S(1)}, u32[]{:S(2)}, u32[]{:S(2)}) collective-permute-start(bf16[96,1152]{1,0:T(8,128)(2,1)S(1)} %get-tuple-element.589), channel_id=1, source_target_pairs={{0,16},{16,0},{1,17},{17,1},{2,18},{18,2},{3,19},{19,3},{4,20},{20... | collective-permute-start | bytes 663560 | tf_op jit(solution)/shard_map/ppermute | solution.py:371
  194.7 9.3 %collective-permute-start.27 = (bf16[2,24,2304]{2,1,0:T(8,128)(2,1)S(1)}, bf16[2,24,2304]{2,1,0:T(8,128)(2,1)S(1)}, u32[]{:S(2)}, u32[]{:S(2)}) collective-permute-start(bf16[2,24,2304]{2,1,0:T(8,128)(2,1)S(1)} %get-tuple-element.627), channel_id=1, source_target_pairs={{0,4},{1,5},{2,6},{3,7},{4,0},{5,1},{6,2},{7,3},{8,12},{9,13},{10,... | collective-permute-start | bytes 663560 | tf_op jit(solution)/shard_map/ppermute | solution.py:385
  214.2 25.7 %collective-permute-start.39 = (bf16[4,2,96,384]{3,2,1,0:T(8,128)(2,1)S(1)}, bf16[4,2,96,384]{3,2,1,0:T(8,128)(2,1)S(1)}, u32[]{:S(2)}, u32[]{:S(2)}) collective-permute-start(bf16[4,2,96,384]{3,2,1,0:T(8,128)(2,1)S(1)} %get-tuple-element.711), channel_id=1, source_target_pairs={{0,2},{1,3},{2,0},{3,1},{4,6},{5,7},{6,4},{7,5},{8,10},{9,11},{10,... | collective-permute-start | bytes 1769480 | tf_op jit(solution)/shard_map/ppermute | solution.py:377
  214.9 25.0 %collective-permute-start.40 = (bf16[4,2,96,384]{3,2,1,0:T(8,128)(2,1)S(1)}, bf16[4,2,96,384]{3,2,1,0:T(8,128)(2,1)S(1)}, u32[]{:S(2)}, u32[]{:S(2)}) collective-permute-start(bf16[4,2,96,384]{3,2,1,0:T(8,128)(2,1)S(1)} %get-tuple-element.713), channel_id=1, source_target_pairs={{0,16},{16,0},{1,17},{17,1},{2,18},{18,2},{3,19},{19,3},{4,20},{20... | collective-permute-start | bytes 1769480 | tf_op jit(solution)/shard_map/ppermute | solution.py:371
  232.2 10.4 %collective-permute-start.37 = (bf16[96,1152]{1,0:T(8,128)(2,1)S(1)}, bf16[96,1152]{1,0:T(8,128)(2,1)S(1)}, u32[]{:S(2)}, u32[]{:S(2)}) collective-permute-start(bf16[96,1152]{1,0:T(8,128)(2,1)S(1)} %get-tuple-element.723.refs_0_), channel_id=1, source_target_pairs={{0,2},{1,3},{2,0},{3,1},{4,6},{5,7},{6,4},{7,5},{8,10},{9,11},{10,... | collective-permute-start | bytes 663560 | tf_op jit(solution)/shard_map/ppermute | solution.py:377
  233.6 9.0 %collective-permute-start.38 = (bf16[96,1152]{1,0:T(8,128)(2,1)S(1)}, bf16[96,1152]{1,0:T(8,128)(2,1)S(1)}, u32[]{:S(2)}, u32[]{:S(2)}) collective-permute-start(bf16[96,1152]{1,0:T(8,128)(2,1)S(1)} %get-tuple-element.725.refs_2_), channel_id=1, source_target_pairs={{0,16},{16,0},{1,17},{17,1},{2,18},{18,2},{3,19},{19,3},{4,20},{20... | collective-permute-start | bytes 663560 | tf_op jit(solution)/shard_map/ppermute | solution.py:371
  241.0 11.8 %collective-permute-start.45 = (bf16[2,2,192,384]{3,2,1,0:T(8,128)(2,1)S(1)}, bf16[2,2,192,384]{3,2,1,0:T(8,128)(2,1)S(1)}, u32[]{:S(2)}, u32[]{:S(2)}) collective-permute-start(bf16[2,2,192,384]{3,2,1,0:T(8,128)(2,1)S(1)} %get-tuple-element.741), channel_id=1, source_target_pairs={{0,4},{1,5},{2,6},{3,7},{4,0},{5,1},{6,2},{7,3},{8,12},{9,13},{10,... | collective-permute-start | bytes 1769480 | tf_op jit(solution)/shard_map/ppermute | solution.py:385
  243.3 10.3 %collective-permute-start.43 = (bf16[192,1152]{1,0:T(8,128)(2,1)S(1)}, bf16[192,1152]{1,0:T(8,128)(2,1)S(1)}, u32[]{:S(2)}, u32[]{:S(2)}) collective-permute-start(bf16[192,1152]{1,0:T(8,128)(2,1)S(1)} %get-tuple-element.749.refs_0_), channel_id=1, source_target_pairs={{0,16},{16,0},{1,17},{17,1},{2,18},{18,2},{3,19},{19,3},{4,20},{20... | collective-permute-start | bytes 1327112 | tf_op jit(solution)/shard_map/ppermute | solution.py:371
  244.7 8.9 %collective-permute-start.44 = (bf16[192,1152]{1,0:T(8,128)(2,1)S(1)}, bf16[192,1152]{1,0:T(8,128)(2,1)S(1)}, u32[]{:S(2)}, u32[]{:S(2)}) collective-permute-start(bf16[192,1152]{1,0:T(8,128)(2,1)S(1)} %get-tuple-element.751.refs_2_), channel_id=1, source_target_pairs={{0,2},{1,3},{2,0},{3,1},{4,6},{5,7},{6,4},{7,5},{8,10},{9,11},{10,... | collective-permute-start | bytes 1327112 | tf_op jit(solution)/shard_map/ppermute | solution.py:377
  254.4 11.3 %collective-permute-start.49 = (bf16[384,2304]{1,0:T(8,128)(2,1)S(1)}, bf16[384,2304]{1,0:T(8,128)(2,1)S(1)}, u32[]{:S(2)}, u32[]{:S(2)}) collective-permute-start(bf16[384,2304]{1,0:T(8,128)(2,1)S(1)} %spread_yx.2.v_ref), channel_id=1, source_target_pairs={{0,1},{1,0},{2,3},{3,2},{4,5},{5,4},{6,7},{7,6},{8,9},{9,8},{10,11... | collective-permute-start | bytes 5308424 | tf_op jit(solution)/shard_map/ppermute | solution.py:377
  255.8 16.3 %collective-permute-start.48 = (bf16[2,192,384]{2,1,0:T(8,128)(2,1)S(1)}, bf16[2,192,384]{2,1,0:T(8,128)(2,1)S(1)}, u32[]{:S(2)}, u32[]{:S(2)}) collective-permute-start(bf16[2,192,384]{2,1,0:T(8,128)(2,1)S(1)} %get-tuple-element.777), channel_id=1, source_target_pairs={{0,8},{1,9},{2,10},{3,11},{4,12},{5,13},{6,14},{7,15},{8,0},{9,1},... | collective-permute-start | bytes 884744 | tf_op jit(solution)/shard_map/ppermute | solution.py:385
  (40 other events, 330.5 us)
where the time goes:
time: 284 us; the launch traced here: 283 us
  Pallas kernels  170 us (60%)
  starting transfers between devices  54.9 us (19%)
  waiting for transfers between devices  47.5 us (17%)
  local copies, waits for them, and re-layouts  6.7 us (2%)
    pallas_call x1, Pallas kernels, ffn(): pl.pallas_call(body, grid_spec=pltpu.PrefetchScalarGridSpec(num_scalar_pr...  39.1 us
    pallas_call x3, Pallas kernels, attend_grad(): pl.pallas_call(attend_grad_body, grid_spec=pltpu.PrefetchScalarGridSpec(n...  35.6 us
    ppermute x27, starting transfers between devices, fetch(): return lax.ppermute(value, 'an', pairs)  24.3 us
    pallas_call x28, Pallas kernels, stage(): pl.pallas_call(body, grid_spec=pltpu.PrefetchScalarGridSpec(num_scalar_pr...  23.8 us
    ppermute x10, waiting for transfers between devices, flip(): return lax.ppermute(value, 'an', pairs)  23.1 us
    pallas_call x3, Pallas kernels, attend(): pl.pallas_call(attend_body, grid=(count, rows), in_specs=specs, out_specs...  21.1 us
    ppermute x10, starting transfers between devices, flip(): return lax.ppermute(value, 'an', pairs)  16.1 us
    pallas_call x4, Pallas kernels, finish(): pl.pallas_call(body, grid_spec=pltpu.PrefetchScalarGridSpec(num_scalar_pr...  15.8 us
  transfers between devices with their start and end apart: 51, of which 18 were waited for; matrix products, arithmetic and copies ran while one was open for 2% of the time, Pallas kernels for 41%

commit v1 on v0

--- a/solution.py
+++ b/solution.py
@@ -391,8 +391,9 @@
         n = self.size[axis]
         return [parts[0]] + [self.fetch(parts[t], axis, n - t) for t in range(1, n)]
 
-    def step(self, fn, arrays, shapes, name, along, steps=1, away=False):
+    def step(self, fn, arrays, shapes, name, along, steps=1, away=False, early=()):
         arrays, along = hold((list(arrays), along))
+        arrays = list(early) + arrays
         return hold((self.stage(fn, arrays, shapes, name, steps, away), along))
 
     def stage(self, fn, arrays, shapes, name, steps, away):
@@ -539,7 +540,9 @@
         return by_distance(cut_rows(v[:, :cut], ny), y) + by_distance(cut_rows(v[:, cut:], nx), x)
 
     shapes = [(rows // ny, cut)] * ny + [(rows // nx, cols - cut)] * nx
-    parts, along = net.step(fn, [own, theirs], shapes, "reduce_yx", along, away=away)
+    parts, along = net.step(
+        fn, [theirs], shapes, "reduce_yx", along, away=away, early=[own]
+    )
     return (net.spread(parts[:ny], "y"), net.spread(parts[ny:], "x")), along
 
 

time: 284 us -> 284 us (level)
  no operation moved by 1% of the time
where the time goes in v1:
time: 284 us; the launch traced here: 283 us
  Pallas kernels  170 us (60%)
  starting transfers between devices  54.9 us (19%)
  waiting for transfers between devices  47.5 us (17%)
  local copies, waits for them, and re-layouts  6.7 us (2%)
    pallas_call x1, Pallas kernels, ffn(): pl.pallas_call(body, grid_spec=pltpu.PrefetchScalarGridSpec(num_scalar_pr...  39.1 us
    pallas_call x3, Pallas kernels, attend_grad(): pl.pallas_call(attend_grad_body, grid_spec=pltpu.PrefetchScalarGridSpec(n...  35.6 us
    ppermute x27, starting transfers between devices, fetch(): return lax.ppermute(value, 'an', pairs)  24.3 us
    pallas_call x28, Pallas kernels, stage(): pl.pallas_call(body, grid_spec=pltpu.PrefetchScalarGridSpec(num_scalar_pr...  23.8 us
    ppermute x10, waiting for transfers between devices, flip(): return lax.ppermute(value, 'an', pairs)  23.1 us
    pallas_call x3, Pallas kernels, attend(): pl.pallas_call(attend_body, grid=(count, rows), in_specs=specs, out_specs...  21.1 us
    ppermute x10, starting transfers between devices, flip(): return lax.ppermute(value, 'an', pairs)  16.1 us
    pallas_call x4, Pallas kernels, finish(): pl.pallas_call(body, grid_spec=pltpu.PrefetchScalarGridSpec(num_scalar_pr...  15.8 us
  transfers between devices with their start and end apart: 51, of which 18 were waited for; matrix products, arithmetic and copies ran while one was open for 2% of the time, Pallas kernels for 41%

profile of v1, /device:TPU:0, one launch (start us, length us, event | category | flops | bytes accessed | tf_op | source)
XLA Modules:
  0.0 282.8 jit_solution(11925032892379034645)
XLA Ops:
  0.7 3.1 %collective-permute-start = (bf16[192,384]{1,0:T(8,128)(2,1)}, bf16[192,384]{1,0:T(8,128)(2,1)S(1)}, u32[]{:S(2)}, u32[]{:S(2)}) collective-permute-start(bf16[192,384]{1,0:T(8,128)(2,1)} %bitcast.38), channel_id=1, source_target_pairs={{0,4},{1,5},{2,6},{3,7},{4,8},{5,9},{6,10},{7,11},{8,12},{9,13},{1... | collective-permute-start | bytes 442376 | tf_op jit(solution)/shard_map/ppermute | solution.py:377
  3.7 2.6 collective-permute-start.1
  11.1 8.2 %project.1 = (bf16[3,1024,768]{2,1,0:T(8,128)(2,1)}, bf16[768,1024]{1,0:T(8,128)(2,1)}) custom-call(bf16[1024,768]{1,0:T(8,128)(2,1)} %bitcast.48, f32[1,768]{1,0:T(1,128)S(1)} %reshape.81.gain_ref.refs_7_, bf16[768,768]{1,0:T(8,128)(2,1)} %wq_ref.7, bf16[768,768]{1,0:T(8,128)(2,1)} %wk_ref.7, bf16[768,768]{1,0:T(8,128)(2,1)} %wv_ref.7), custom_call_target="tpu_custom_call" | custom-call | flops 1000 | bytes 1000 | tf_op jit(solution)/shard_map/project/pallas_call | solution.py:709
  23.4 7.1 %attend.3 = (bf16[12,2,512,512]{3,2,1,0:T(8,128)(2,1)}, f32[12,2,512]{2,1,0:T(2,128)S(1)}, bf16[1024,768]{1,0:T(8,128)(2,1)S(1)}, bf16[768,1024]{1,0:T(8,128)(2,1)S(1)}) custom-call(bf16[3,1024,768]{2,1,0:T(8,128)(2,1)} %get-tuple-element.463.p_ref, bf16[1024,128]{1,0:T(8,128)(2,1)S(1)} %fusion.kseg_ref, bf16[1024,128]{1,0:T(8,128)(2,1)S(1)} %select_convert_fusion.qseg_ref, ...), custom_call_target="tpu_custom_call" | custom-call | flops 1000 | bytes 1000 | tf_op jit(solution)/shard_map/attend/pallas_call | solution.py:125
  36.1 7.0 %attend.4 = (bf16[12,2,512,512]{3,2,1,0:T(8,128)(2,1)}, f32[12,2,512]{2,1,0:T(2,128)S(1)}, bf16[1024,768]{1,0:T(8,128)(2,1)S(1)}, bf16[768,1024]{1,0:T(8,128)(2,1)S(1)}) custom-call(bf16[3,1024,768]{2,1,0:T(8,128)(2,1)} %get-tuple-element.463.p_ref, ...), custom_call_target="tpu_custom_call", output_to_operand_aliasing={{0}: (4, {}), {1}: (5, {}), {2}: (6, {}), {3}: (7, {})} | custom-call | flops 1000 | bytes 1000 | tf_op jit(solution)/shard_map/attend/pallas_call | solution.py:125
  47.9 7.0 %attend.5 = (bf16[12,2,512,512]{3,2,1,0:T(8,128)(2,1)}, f32[12,2,512]{2,1,0:T(2,128)S(1)}, bf16[1024,768]{1,0:T(8,128)(2,1)S(1)}, bf16[768,1024]{1,0:T(8,128)(2,1)S(1)}) custom-call(bf16[3,1024,768]{2,1,0:T(8,128)(2,1)} %get-tuple-element.463.p_ref, ...), custom_call_target="tpu_custom_call", output_to_operand_aliasing={{0}: (4, {}), {1}: (5, {}), {2}: (6, {}), {3}: (7, {})} | custom-call | flops 1000 | bytes 1000 | tf_op jit(solution)/shard_map/attend/pallas_call | solution.py:125
  57.7 6.5 %before_ffn.1 = (bf16[1024,768]{1,0:T(8,128)(2,1)}, bf16[1024,768]{1,0:T(8,128)(2,1)}, bf16[768,1024]{1,0:T(8,128)(2,1)}, bf16[768,1024]{1,0:T(8,128)(2,1)}) custom-call(bf16[1024,768]{1,0:T(8,128)(2,1)S(1)} %get-tuple-element.499.mixed_ref.o_ref, bf16[768,768]{1,0:T(8,128)(2,1)} %w_ref.3, bf16[1024,768]{1,0:T(8,128)(2,1)} %bitcast.49, ...), custom_call_target="tpu_custom_call" | custom-call | flops 1000 | bytes 1000 | tf_op jit(solution)/shard_map/before_ffn/pallas_call | solution.py:758
  64.3 6.8 %collective-permute-done.13.refs_1_ = bf16[4,2,96,384]{3,2,1,0:T(8,128)(2,1)S(1)} collective-permute-done((bf16[4,2,96,384]{3,2,1,0:T(8,128)(2,1)S(1)}, bf16[4,2,96,384]{3,2,1,0:T(8,128)(2,1)S(1)}, u32[]{:S(2)}, u32[]{:S(2)}) %collective-permute-start.13) | collective-permute-done | bytes 589856 | tf_op jit(solution)/shard_map/ppermute | solution.py:371
  72.2 4.5 %collective-permute-done.15.d1_ref = bf16[4,2,192,768]{3,2,1,0:T(8,128)(2,1)S(1)} collective-permute-done((bf16[4,2,192,768]{3,2,1,0:T(8,128)(2,1)S(1)}, bf16[4,2,192,768]{3,2,1,0:T(8,128)(2,1)S(1)}, u32[]{:S(2)}, u32[]{:S(2)}) %collective-permute-start.15) | collective-permute-done | bytes 2359328 | tf_op jit(solution)/shard_map/ppermute | solution.py:377
  76.7 39.1 %ffn.1 = (bf16[1024,768]{1,0:T(8,128)(2,1)}, bf16[4,2,2,192,768]{4,3,2,1,0:T(8,128)(2,1)}, bf16[4,2,2,192,768]{4,3,2,1,0:T(8,128)(2,1)}, bf16[1024,768]{1,0:T(8,128)(2,1)}) custom-call(s32[4]{0:T(128)S(1)} %pad_add_fusion.place_ref, bf16[4,2,192,768]{3,2,1,0:T(8,128)(2,1)S(1)} %gather_yx.2.u0_ref, ...), custom_call_target="tpu_custom_call" | custom-call | flops 1000 | bytes 1000 | tf_op jit(solution)/shard_map/ffn/pallas_call | solution.py:872
  116.0 10.0 %after_ffn.1 = (bf16[1024,768]{1,0:T(8,128)(2,1)}, bf16[1024,768]{1,0:T(8,128)(2,1)S(1)}, f32[1,768]{1,0:T(1,128)S(1)}, bf16[384,2304]{1,0:T(8,128)(2,1)}, bf16[384,2304]{1,0:T(8,128)(2,1)}) custom-call(s32[4]{0:T(128)S(1)} %pad_add_fusion.place_ref, bf16[1024,768]{1,0:T(8,128)(2,1)} %get-tuple-element.521.gs_ref, ...), custom_call_target="tpu_custom_call" | custom-call | flops 1000 | bytes 1000 | tf_op jit(solution)/shard_map/after_ffn/pallas_call | solution.py:953
  126.1 2.1 scatter_yx.1
  130.4 11.8 %attend_grad.3 = (bf16[1024,768]{1,0:T(8,128)(2,1)}, f32[4,2,768]{2,1,0:T(2,128)S(1)}, bf16[384,2304]{1,0:T(8,128)(2,1)}, bf16[384,2304]{1,0:T(8,128)(2,1)}) custom-call(s32[4]{0:T(128)S(1)} %pad_add_fusion.place_ref, bf16[3,1024,768]{2,1,0:T(8,128)(2,1)} %get-tuple-element.463.p_ref, ...), custom_call_target="tpu_custom_call", output_to_operand_aliasing={{2}: (8, {}), {3}: (9, {})} | custom-call | flops 1000 | bytes 1000 | tf_op jit(solution)/shard_map/attend_grad/pallas_call | solution.py:286
  142.3 11.9 %attend_grad.4 = (bf16[1024,768]{1,0:T(8,128)(2,1)}, f32[4,2,768]{2,1,0:T(2,128)S(1)}, bf16[384,2304]{1,0:T(8,128)(2,1)}, bf16[384,2304]{1,0:T(8,128)(2,1)}) custom-call(s32[4]{0:T(128)S(1)} %pad_add_fusion.place_ref, bf16[3,1024,768]{2,1,0:T(8,128)(2,1)} %get-tuple-element.463.p_ref, ...), custom_call_target="tpu_custom_call", output_to_operand_aliasing={{2}: (8, {}), {3}: (9, {})} | custom-call | flops 1000 | bytes 1000 | tf_op jit(solution)/shard_map/attend_grad/pallas_call | solution.py:286
  154.2 2.1 collective-permute-done.17.refs_1_
  157.6 3.9 %collective-permute-done.19.refs_1_ = bf16[384,2304]{1,0:T(8,128)(2,1)S(1)} collective-permute-done((bf16[384,2304]{1,0:T(8,128)(2,1)}, bf16[384,2304]{1,0:T(8,128)(2,1)S(1)}, u32[]{:S(2)}, u32[]{:S(2)}) %collective-permute-start.19) | collective-permute-done | bytes 1769504 | tf_op jit(solution)/shard_map/ppermute | solution.py:377
  163.0 2.0 reduce_yx.2
  166.0 11.9 %attend_grad.5 = (bf16[1024,768]{1,0:T(8,128)(2,1)}, f32[4,2,768]{2,1,0:T(2,128)S(1)}, bf16[384,896]{1,0:T(8,128)(2,1)}, bf16[384,896]{1,0:T(8,128)(2,1)}) custom-call(s32[4]{0:T(128)S(1)} %pad_add_fusion.place_ref, bf16[3,1024,768]{2,1,0:T(8,128)(2,1)} %get-tuple-element.463.p_ref, bf16[12,2,512,512]{3,2,1,0:T(8,128)(2,1)} %get-tuple-element.532.u_ref, ...), custom_call_target="tpu_custom_call" | custom-call | flops 1000 | bytes 1000 | tf_op jit(solution)/shard_map/attend_grad/pallas_call | solution.py:286
  177.9 2.0 reduce_xy.2
  184.3 9.6 %token_grad.1 = f32[1024,768]{1,0:T(8,128)} custom-call(bf16[1024,768]{1,0:T(8,128)(2,1)} %get-tuple-element.598.refs_0_, bf16[1024,768]{1,0:T(8,128)(2,1)} %get-tuple-element.599.refs_1_, bf16[1024,768]{1,0:T(8,128)(2,1)} %get-tuple-element.600.refs_2_, bf16[768,768]{1,0:T(8,128)(2,1)} %wq_ref.7, bf16[768,768]{1,0:T(8,128)(2,1)} %wk_ref.7, ...), custom_call_target="tpu_custom_call" | custom-call | flops 1000 | bytes 1000 | tf_op jit(solution)/shard_map/token_grad/pallas_call | solution.py:1009
  194.7 3.8 %collective-permute-start.27 = (bf16[2,24,2304]{2,1,0:T(8,128)(2,1)S(1)}, bf16[2,24,2304]{2,1,0:T(8,128)(2,1)S(1)}, u32[]{:S(2)}, u32[]{:S(2)}) collective-permute-start(bf16[2,24,2304]{2,1,0:T(8,128)(2,1)S(1)} %get-tuple-element.623), channel_id=1, source_target_pairs={{0,4},{1,5},{2,6},{3,7},{4,0},{5,1},{6,2},{7,3},{8,12},{9,13},{10,... | collective-permute-start | bytes 663560 | tf_op jit(solution)/shard_map/ppermute | solution.py:385
  200.4 3.5 %collective-permute-done.27.refs_1_ = bf16[2,24,2304]{2,1,0:T(8,128)(2,1)S(1)} collective-permute-done((bf16[2,24,2304]{2,1,0:T(8,128)(2,1)S(1)}, bf16[2,24,2304]{2,1,0:T(8,128)(2,1)S(1)}, u32[]{:S(2)}, u32[]{:S(2)}) %collective-permute-start.27) | collective-permute-done | bytes 221216 | tf_op jit(solution)/shard_map/ppermute | solution.py:385
  207.9 3.7 %collective-permute-done.28.refs_1_ = bf16[96,384]{1,0:T(8,128)(2,1)S(1)} collective-permute-done((bf16[96,384]{1,0:T(8,128)(2,1)S(1)}, bf16[96,384]{1,0:T(8,128)(2,1)S(1)}, u32[]{:S(2)}, u32[]{:S(2)}) %collective-permute-start.28) | collective-permute-done | bytes 73760 | tf_op jit(solution)/shard_map/ppermute | solution.py:377
  219.6 4.3 %collective-permute-done.30.refs_1_ = bf16[2,24,896]{2,1,0:T(8,128)(2,1)S(1)} collective-permute-done((bf16[2,24,896]{2,1,0:T(8,128)(2,1)S(1)}, bf16[2,24,896]{2,1,0:T(8,128)(2,1)S(1)}, u32[]{:S(2)}, u32[]{:S(2)}) %collective-permute-start.30) | collective-permute-done | bytes 86048 | tf_op jit(solution)/shard_map/ppermute | solution.py:385
  226.9 3.8 %collective-permute-done.32.refs_1_ = bf16[24,896]{1,0:T(8,128)(2,1)S(1)} collective-permute-done((bf16[24,896]{1,0:T(8,128)(2,1)S(1)}, bf16[24,896]{1,0:T(8,128)(2,1)S(1)}, u32[]{:S(2)}, u32[]{:S(2)}) %collective-permute-start.32) | collective-permute-done | bytes 43040 | tf_op jit(solution)/shard_map/ppermute | solution.py:385
  236.2 3.1 %collective-permute-done.34.refs_1_ = bf16[24,896]{1,0:T(8,128)(2,1)S(1)} collective-permute-done((bf16[24,896]{1,0:T(8,128)(2,1)S(1)}, bf16[24,896]{1,0:T(8,128)(2,1)S(1)}, u32[]{:S(2)}, u32[]{:S(2)}) %collective-permute-start.34) | collective-permute-done | bytes 43040 | tf_op jit(solution)/shard_map/ppermute | solution.py:385
  245.9 6.4 %collective-permute-done.36.refs_1_ = bf16[2,24,896]{2,1,0:T(8,128)(2,1)S(1)} collective-permute-done((bf16[2,24,896]{2,1,0:T(8,128)(2,1)S(1)}, bf16[2,24,896]{2,1,0:T(8,128)(2,1)S(1)}, u32[]{:S(2)}, u32[]{:S(2)}) %collective-permute-start.36) | collective-permute-done | bytes 86048 | tf_op jit(solution)/shard_map/ppermute | solution.py:385
  255.8 2.4 collective-permute-start.48
  258.6 4.4 %finish.4 = (f32[768,768]{1,0:T(8,128)}, f32[768,768]{1,0:T(8,128)}, f32[768,768]{1,0:T(8,128)}, f32[768,768]{1,0:T(8,128)}, f32[1,768]{1,0:T(1,128)S(1)}) custom-call(s32[4]{0:T(128)S(1)} %pad_add_fusion.place_ref, bf16[384,2304]{1,0:T(8,128)(2,1)S(1)} %spread_yx.2.v_ref, bf16[768,768]{1,0:T(8,128)(2,1)} %wq_ref.7, bf16[768,768]{1,0:T(8,128)(2,1)} %wk_ref.7, ...), custom_call_target="tpu_custom_call" | custom-call | flops 1000 | bytes 1000 | tf_op jit(solution)/shard_map/finish/pallas_call | solution.py:670
  265.7 4.4 %finish.5 = (f32[768,768]{1,0:T(8,128)}, f32[768,768]{1,0:T(8,128)}, f32[768,768]{1,0:T(8,128)}, f32[768,768]{1,0:T(8,128)}, f32[1,768]{1,0:T(1,128)S(1)}) custom-call(s32[4]{0:T(128)S(1)} %pad_add_fusion.place_ref, ...), custom_call_target="tpu_custom_call", output_to_operand_aliasing={{0}: (6, {}), {1}: (7, {}), {2}: (8, {}), {3}: (9, {}), {4}... | custom-call | flops 1000 | bytes 1000 | tf_op jit(solution)/shard_map/finish/pallas_call | solution.py:670
  272.8 3.5 %finish.6 = (f32[768,768]{1,0:T(8,128)}, f32[768,768]{1,0:T(8,128)}, f32[768,768]{1,0:T(8,128)}, f32[8,768]{1,0:T(8,128)S(1)}, f32[1,768]{1,0:T(1,128)S(1)}) custom-call(s32[4]{0:T(128)S(1)} %pad_add_fusion.place_ref, bf16[384,896]{1,0:T(8,128)(2,1)S(1)} %spread_yx.3.v_ref, ...), custom_call_target="tpu_custom_call", output_to_operand_aliasing={{0}: (7, {}), {1}: (8, {}), {2}: (9, {})} | custom-call | flops 1000 | bytes 1000 | tf_op jit(solution)/shard_map/finish/pallas_call | solution.py:670
  277.2 3.5 %finish.7 = (f32[768,768]{1,0:T(8,128)}, f32[768,768]{1,0:T(8,128)}, f32[768,768]{1,0:T(8,128)}, f32[8,768]{1,0:T(8,128)S(1)}, f32[1,768]{1,0:T(1,128)S(1)}) custom-call(s32[4]{0:T(128)S(1)} %pad_add_fusion.place_ref, ...), custom_call_target="tpu_custom_call", output_to_operand_aliasing={{0}: (7, {}), {1}: (8, {}), {2}: (9, {}), {3}: (10, {}), {4... | custom-call | flops 1000 | bytes 1000 | tf_op jit(solution)/shard_map/finish/pallas_call | solution.py:670
  (187 shorter events, 75.6 us)
Async XLA Ops:
  0.7 18.8 %collective-permute-start = (bf16[192,384]{1,0:T(8,128)(2,1)}, bf16[192,384]{1,0:T(8,128)(2,1)S(1)}, u32[]{:S(2)}, u32[]{:S(2)}) collective-permute-start(bf16[192,384]{1,0:T(8,128)(2,1)} %bitcast.38), channel_id=1, source_target_pairs={{0,4},{1,5},{2,6},{3,7},{4,8},{5,9},{6,10},{7,11},{8,12},{9,13},{1... | collective-permute-start | bytes 442376 | tf_op jit(solution)/shard_map/ppermute | solution.py:377
  3.7 15.7 %collective-permute-start.1 = (bf16[192,384]{1,0:T(8,128)(2,1)}, bf16[192,384]{1,0:T(8,128)(2,1)S(1)}, u32[]{:S(2)}, u32[]{:S(2)}) collective-permute-start(bf16[192,384]{1,0:T(8,128)(2,1)} %bitcast.39), channel_id=1, source_target_pairs={{0,8},{1,9},{2,10},{3,11},{4,12},{5,13},{6,14},{7,15},{8,0},{9,1},... | collective-permute-start | bytes 442376 | tf_op jit(solution)/shard_map/ppermute | solution.py:377
  6.3 13.1 %collective-permute-start.2 = (bf16[192,384]{1,0:T(8,128)(2,1)}, bf16[192,384]{1,0:T(8,128)(2,1)S(1)}, u32[]{:S(2)}, u32[]{:S(2)}) collective-permute-start(bf16[192,384]{1,0:T(8,128)(2,1)} %bitcast.40), channel_id=1, source_target_pairs={{0,12},{1,13},{2,14},{3,15},{4,0},{5,1},{6,2},{7,3},{8,4},{9,5},{1... | collective-permute-start | bytes 442376 | tf_op jit(solution)/shard_map/ppermute | solution.py:377
  20.1 10.4 %collective-permute-start.3 = (bf16[4,96,384]{2,1,0:T(8,128)(2,1)S(1)}, bf16[4,96,384]{2,1,0:T(8,128)(2,1)S(1)}, u32[]{:S(2)}, u32[]{:S(2)}) collective-permute-start(bf16[4,96,384]{2,1,0:T(8,128)(2,1)S(1)} %get-tuple-element.429.refs_0_), channel_id=1, source_target_pairs={{0,2},{1,3},{2,0},{3,1},{4,6},{5,7},{6,4},{7,5},{8,10},{9,11},{10,... | collective-permute-start | bytes 884744 | tf_op jit(solution)/shard_map/ppermute | solution.py:377
  31.2 23.7 %collective-permute-start.5 = (bf16[4,2,96,384]{3,2,1,0:T(8,128)(2,1)S(1)}, bf16[4,2,96,384]{3,2,1,0:T(8,128)(2,1)S(1)}, u32[]{:S(2)}, u32[]{:S(2)}) collective-permute-start(bf16[4,2,96,384]{3,2,1,0:T(8,128)(2,1)S(1)} %get-tuple-element.472.refs_0_), channel_id=1, source_target_pairs={{0,16},{16,0},{1,17},{17,1},{2,18},{18,2},{3,19},{19,3},{4,20},{20... | collective-permute-start | bytes 1769480 | tf_op jit(solution)/shard_map/ppermute | solution.py:371
  31.8 23.2 %collective-permute-start.6 = (bf16[4,96,768]{2,1,0:T(8,128)(2,1)S(1)}, bf16[4,96,768]{2,1,0:T(8,128)(2,1)S(1)}, u32[]{:S(2)}, u32[]{:S(2)}) collective-permute-start(bf16[4,96,768]{2,1,0:T(8,128)(2,1)S(1)} %get-tuple-element.474.refs_2_), channel_id=1, source_target_pairs={{0,2},{1,3},{2,0},{3,1},{4,6},{5,7},{6,4},{7,5},{8,10},{9,11},{10,... | collective-permute-start | bytes 1769480 | tf_op jit(solution)/shard_map/ppermute | solution.py:377
  32.3 10.8 %collective-permute-start.7 = (bf16[192,384]{1,0:T(8,128)(2,1)S(1)}, bf16[192,384]{1,0:T(8,128)(2,1)S(1)}, u32[]{:S(2)}, u32[]{:S(2)}) collective-permute-start(bf16[192,384]{1,0:T(8,128)(2,1)S(1)} %copy-done.15), channel_id=1, source_target_pairs={{0,4},{1,5},{2,6},{3,7},{4,8},{5,9},{6,10},{7,11},{8,12},{9,13},{1... | collective-permute-start | bytes 442376 | tf_op jit(solution)/shard_map/ppermute | solution.py:377
  33.5 10.7 %collective-permute-start.8 = (bf16[192,384]{1,0:T(8,128)(2,1)S(1)}, bf16[192,384]{1,0:T(8,128)(2,1)S(1)}, u32[]{:S(2)}, u32[]{:S(2)}) collective-permute-start(bf16[192,384]{1,0:T(8,128)(2,1)S(1)} %copy-done.15), channel_id=1, source_target_pairs={{0,8},{1,9},{2,10},{3,11},{4,12},{5,13},{6,14},{7,15},{8,0},{9,1},... | collective-permute-start | bytes 442376 | tf_op jit(solution)/shard_map/ppermute | solution.py:377
  34.3 9.9 %collective-permute-start.9 = (bf16[192,384]{1,0:T(8,128)(2,1)S(1)}, bf16[192,384]{1,0:T(8,128)(2,1)S(1)}, u32[]{:S(2)}, u32[]{:S(2)}) collective-permute-start(bf16[192,384]{1,0:T(8,128)(2,1)S(1)} %copy-done.15), channel_id=1, source_target_pairs={{0,12},{1,13},{2,14},{3,15},{4,0},{5,1},{6,2},{7,3},{8,4},{9,5},{1... | collective-permute-start | bytes 442376 | tf_op jit(solution)/shard_map/ppermute | solution.py:377
  44.9 10.9 %collective-permute-start.11 = (bf16[4,96,384]{2,1,0:T(8,128)(2,1)S(1)}, bf16[4,96,384]{2,1,0:T(8,128)(2,1)S(1)}, u32[]{:S(2)}, u32[]{:S(2)}) collective-permute-start(bf16[4,96,384]{2,1,0:T(8,128)(2,1)S(1)} %get-tuple-element.487.refs_0_), channel_id=1, source_target_pairs={{0,2},{1,3},{2,0},{3,1},{4,6},{5,7},{6,4},{7,5},{8,10},{9,11},{10,... | collective-permute-start | bytes 884744 | tf_op jit(solution)/shard_map/ppermute | solution.py:377
  46.4 9.3 %collective-permute-start.12 = (bf16[4,96,384]{2,1,0:T(8,128)(2,1)S(1)}, bf16[4,96,384]{2,1,0:T(8,128)(2,1)S(1)}, u32[]{:S(2)}, u32[]{:S(2)}) collective-permute-start(bf16[4,96,384]{2,1,0:T(8,128)(2,1)S(1)} %get-tuple-element.489.refs_2_), channel_id=1, source_target_pairs={{0,16},{16,0},{1,17},{17,1},{2,18},{18,2},{3,19},{19,3},{4,20},{20... | collective-permute-start | bytes 884744 | tf_op jit(solution)/shard_map/ppermute | solution.py:371
  56.5 14.6 %collective-permute-start.13 = (bf16[4,2,96,384]{3,2,1,0:T(8,128)(2,1)S(1)}, bf16[4,2,96,384]{3,2,1,0:T(8,128)(2,1)S(1)}, u32[]{:S(2)}, u32[]{:S(2)}) collective-permute-start(bf16[4,2,96,384]{3,2,1,0:T(8,128)(2,1)S(1)} %get-tuple-element.501.refs_0_), channel_id=1, source_target_pairs={{0,16},{16,0},{1,17},{17,1},{2,18},{18,2},{3,19},{19,3},{4,20},{20... | collective-permute-start | bytes 1769480 | tf_op jit(solution)/shard_map/ppermute | solution.py:371
  57.2 14.1 %collective-permute-start.14 = (bf16[4,96,768]{2,1,0:T(8,128)(2,1)S(1)}, bf16[4,96,768]{2,1,0:T(8,128)(2,1)S(1)}, u32[]{:S(2)}, u32[]{:S(2)}) collective-permute-start(bf16[4,96,768]{2,1,0:T(8,128)(2,1)S(1)} %get-tuple-element.503.refs_2_), channel_id=1, source_target_pairs={{0,2},{1,3},{2,0},{3,1},{4,6},{5,7},{6,4},{7,5},{8,10},{9,11},{10,... | collective-permute-start | bytes 1769480 | tf_op jit(solution)/shard_map/ppermute | solution.py:377
  57.7 14.5 %collective-permute-start.10 = (bf16[4,2,192,768]{3,2,1,0:T(8,128)(2,1)S(1)}, bf16[4,2,192,768]{3,2,1,0:T(8,128)(2,1)S(1)}, u32[]{:S(2)}, u32[]{:S(2)}) collective-permute-start(bf16[4,2,192,768]{3,2,1,0:T(8,128)(2,1)S(1)} %gather_yx.2.u0_ref), channel_id=1, source_target_pairs={{0,1},{1,0},{2,3},{3,2},{4,5},{5,4},{6,7},{7,6},{8,9},{9,8},{10,11... | collective-permute-start | bytes 7077896 | tf_op jit(solution)/shard_map/ppermute | solution.py:377
  115.8 10.2 %collective-permute-start.16 = (bf16[4,2,2,192,768]{4,3,2,1,0:T(8,128)(2,1)}, bf16[4,2,2,192,768]{4,3,2,1,0:T(8,128)(2,1)S(1)}, u32[]{:S(2)}, u32[]{:S(2)}) collective-permute-start(bf16[4,2,2,192,768]{4,3,2,1,0:T(8,128)(2,1)} %get-tuple-element.520), channel_id=1, source_target_pairs={{0,1},{1,0},{2,3},{3,2},{4,5},{5,4},{6,7},{7,6},{8,9},{9,8},{10,11... | collective-permute-start | bytes 14155784 | tf_op jit(solution)/shard_map/ppermute | solution.py:377
  128.2 28.1 %collective-permute-start.17 = (bf16[4,2,2,96,384]{4,3,2,1,0:T(8,128)(2,1)S(1)}, bf16[4,2,2,96,384]{4,3,2,1,0:T(8,128)(2,1)S(1)}, u32[]{:S(2)}, u32[]{:S(2)}) collective-permute-start(bf16[4,2,2,96,384]{4,3,2,1,0:T(8,128)(2,1)S(1)} %get-tuple-element.542), channel_id=1, source_target_pairs={{0,16},{16,0},{1,17},{17,1},{2,18},{18,2},{3,19},{19,3},{4,20},{20... | collective-permute-start | bytes 3538952 | tf_op jit(solution)/shard_map/ppermute | solution.py:371
  129.9 27.7 %collective-permute-start.18 = (bf16[4,2,96,768]{3,2,1,0:T(8,128)(2,1)S(1)}, bf16[4,2,96,768]{3,2,1,0:T(8,128)(2,1)S(1)}, u32[]{:S(2)}, u32[]{:S(2)}) collective-permute-start(bf16[4,2,96,768]{3,2,1,0:T(8,128)(2,1)S(1)} %get-tuple-element.544), channel_id=1, source_target_pairs={{0,2},{1,3},{2,0},{3,1},{4,6},{5,7},{6,4},{7,5},{8,10},{9,11},{10,... | collective-permute-start | bytes 3538952 | tf_op jit(solution)/shard_map/ppermute | solution.py:377
  165.0 12.9 %collective-permute-start.20 = (bf16[192,1152]{1,0:T(8,128)(2,1)}, bf16[192,1152]{1,0:T(8,128)(2,1)}, u32[]{:S(2)}, u32[]{:S(2)}) collective-permute-start(bf16[192,1152]{1,0:T(8,128)(2,1)} %get-tuple-element.555), channel_id=1, source_target_pairs={{0,16},{16,0},{1,17},{17,1},{2,18},{18,2},{3,19},{19,3},{4,20},{20... | collective-permute-start | bytes 1327112 | tf_op jit(solution)/shard_map/ppermute | solution.py:371
  165.4 12.5 %collective-permute-start.21 = (bf16[192,1152]{1,0:T(8,128)(2,1)}, bf16[192,1152]{1,0:T(8,128)(2,1)}, u32[]{:S(2)}, u32[]{:S(2)}) collective-permute-start(bf16[192,1152]{1,0:T(8,128)(2,1)} %get-tuple-element.557), channel_id=1, source_target_pairs={{0,2},{1,3},{2,0},{3,1},{4,6},{5,7},{6,4},{7,5},{8,10},{9,11},{10,... | collective-permute-start | bytes 1327112 | tf_op jit(solution)/shard_map/ppermute | solution.py:377
  181.1 17.4 %collective-permute-start.24 = (bf16[384,896]{1,0:T(8,128)(2,1)S(1)}, bf16[384,896]{1,0:T(8,128)(2,1)S(1)}, u32[]{:S(2)}, u32[]{:S(2)}) collective-permute-start(bf16[384,896]{1,0:T(8,128)(2,1)S(1)} %get-tuple-element.597), channel_id=1, source_target_pairs={{0,1},{1,0},{2,3},{3,2},{4,5},{5,4},{6,7},{7,6},{8,9},{9,8},{10,11... | collective-permute-start | bytes 2064392 | tf_op jit(solution)/shard_map/ppermute | solution.py:377
  181.2 12.7 %collective-permute-start.22 = (bf16[96,1152]{1,0:T(8,128)(2,1)S(1)}, bf16[96,1152]{1,0:T(8,128)(2,1)S(1)}, u32[]{:S(2)}, u32[]{:S(2)}) collective-permute-start(bf16[96,1152]{1,0:T(8,128)(2,1)S(1)} %get-tuple-element.584), channel_id=1, source_target_pairs={{0,2},{1,3},{2,0},{3,1},{4,6},{5,7},{6,4},{7,5},{8,10},{9,11},{10,... | collective-permute-start | bytes 663560 | tf_op jit(solution)/shard_map/ppermute | solution.py:377
  182.7 11.2 %collective-permute-start.23 = (bf16[96,1152]{1,0:T(8,128)(2,1)S(1)}, bf16[96,1152]{1,0:T(8,128)(2,1)S(1)}, u32[]{:S(2)}, u32[]{:S(2)}) collective-permute-start(bf16[96,1152]{1,0:T(8,128)(2,1)S(1)} %get-tuple-element.586), channel_id=1, source_target_pairs={{0,16},{16,0},{1,17},{17,1},{2,18},{18,2},{3,19},{19,3},{4,20},{20... | collective-permute-start | bytes 663560 | tf_op jit(solution)/shard_map/ppermute | solution.py:371
  194.7 9.3 %collective-permute-start.27 = (bf16[2,24,2304]{2,1,0:T(8,128)(2,1)S(1)}, bf16[2,24,2304]{2,1,0:T(8,128)(2,1)S(1)}, u32[]{:S(2)}, u32[]{:S(2)}) collective-permute-start(bf16[2,24,2304]{2,1,0:T(8,128)(2,1)S(1)} %get-tuple-element.623), channel_id=1, source_target_pairs={{0,4},{1,5},{2,6},{3,7},{4,0},{5,1},{6,2},{7,3},{8,12},{9,13},{10,... | collective-permute-start | bytes 663560 | tf_op jit(solution)/shard_map/ppermute | solution.py:385
  214.2 25.7 %collective-permute-start.39 = (bf16[4,2,96,384]{3,2,1,0:T(8,128)(2,1)S(1)}, bf16[4,2,96,384]{3,2,1,0:T(8,128)(2,1)S(1)}, u32[]{:S(2)}, u32[]{:S(2)}) collective-permute-start(bf16[4,2,96,384]{3,2,1,0:T(8,128)(2,1)S(1)} %get-tuple-element.707), channel_id=1, source_target_pairs={{0,2},{1,3},{2,0},{3,1},{4,6},{5,7},{6,4},{7,5},{8,10},{9,11},{10,... | collective-permute-start | bytes 1769480 | tf_op jit(solution)/shard_map/ppermute | solution.py:377
  214.9 25.0 %collective-permute-start.40 = (bf16[4,2,96,384]{3,2,1,0:T(8,128)(2,1)S(1)}, bf16[4,2,96,384]{3,2,1,0:T(8,128)(2,1)S(1)}, u32[]{:S(2)}, u32[]{:S(2)}) collective-permute-start(bf16[4,2,96,384]{3,2,1,0:T(8,128)(2,1)S(1)} %get-tuple-element.709), channel_id=1, source_target_pairs={{0,16},{16,0},{1,17},{17,1},{2,18},{18,2},{3,19},{19,3},{4,20},{20... | collective-permute-start | bytes 1769480 | tf_op jit(solution)/shard_map/ppermute | solution.py:371
  232.2 10.4 %collective-permute-start.37 = (bf16[96,1152]{1,0:T(8,128)(2,1)S(1)}, bf16[96,1152]{1,0:T(8,128)(2,1)S(1)}, u32[]{:S(2)}, u32[]{:S(2)}) collective-permute-start(bf16[96,1152]{1,0:T(8,128)(2,1)S(1)} %get-tuple-element.719.refs_0_), channel_id=1, source_target_pairs={{0,2},{1,3},{2,0},{3,1},{4,6},{5,7},{6,4},{7,5},{8,10},{9,11},{10,... | collective-permute-start | bytes 663560 | tf_op jit(solution)/shard_map/ppermute | solution.py:377
  233.6 9.0 %collective-permute-start.38 = (bf16[96,1152]{1,0:T(8,128)(2,1)S(1)}, bf16[96,1152]{1,0:T(8,128)(2,1)S(1)}, u32[]{:S(2)}, u32[]{:S(2)}) collective-permute-start(bf16[96,1152]{1,0:T(8,128)(2,1)S(1)} %get-tuple-element.721.refs_2_), channel_id=1, source_target_pairs={{0,16},{16,0},{1,17},{17,1},{2,18},{18,2},{3,19},{19,3},{4,20},{20... | collective-permute-start | bytes 663560 | tf_op jit(solution)/shard_map/ppermute | solution.py:371
  241.0 11.8 %collective-permute-start.45 = (bf16[2,2,192,384]{3,2,1,0:T(8,128)(2,1)S(1)}, bf16[2,2,192,384]{3,2,1,0:T(8,128)(2,1)S(1)}, u32[]{:S(2)}, u32[]{:S(2)}) collective-permute-start(bf16[2,2,192,384]{3,2,1,0:T(8,128)(2,1)S(1)} %get-tuple-element.737), channel_id=1, source_target_pairs={{0,4},{1,5},{2,6},{3,7},{4,0},{5,1},{6,2},{7,3},{8,12},{9,13},{10,... | collective-permute-start | bytes 1769480 | tf_op jit(solution)/shard_map/ppermute | solution.py:385
  243.3 10.3 %collective-permute-start.43 = (bf16[192,1152]{1,0:T(8,128)(2,1)S(1)}, bf16[192,1152]{1,0:T(8,128)(2,1)S(1)}, u32[]{:S(2)}, u32[]{:S(2)}) collective-permute-start(bf16[192,1152]{1,0:T(8,128)(2,1)S(1)} %get-tuple-element.745.refs_0_), channel_id=1, source_target_pairs={{0,16},{16,0},{1,17},{17,1},{2,18},{18,2},{3,19},{19,3},{4,20},{20... | collective-permute-start | bytes 1327112 | tf_op jit(solution)/shard_map/ppermute | solution.py:371
  244.7 8.9 %collective-permute-start.44 = (bf16[192,1152]{1,0:T(8,128)(2,1)S(1)}, bf16[192,1152]{1,0:T(8,128)(2,1)S(1)}, u32[]{:S(2)}, u32[]{:S(2)}) collective-permute-start(bf16[192,1152]{1,0:T(8,128)(2,1)S(1)} %get-tuple-element.747.refs_2_), channel_id=1, source_target_pairs={{0,2},{1,3},{2,0},{3,1},{4,6},{5,7},{6,4},{7,5},{8,10},{9,11},{10,... | collective-permute-start | bytes 1327112 | tf_op jit(solution)/shard_map/ppermute | solution.py:377
  254.4 11.3 %collective-permute-start.49 = (bf16[384,2304]{1,0:T(8,128)(2,1)S(1)}, bf16[384,2304]{1,0:T(8,128)(2,1)S(1)}, u32[]{:S(2)}, u32[]{:S(2)}) collective-permute-start(bf16[384,2304]{1,0:T(8,128)(2,1)S(1)} %spread_yx.2.v_ref), channel_id=1, source_target_pairs={{0,1},{1,0},{2,3},{3,2},{4,5},{5,4},{6,7},{7,6},{8,9},{9,8},{10,11... | collective-permute-start | bytes 5308424 | tf_op jit(solution)/shard_map/ppermute | solution.py:377
  255.8 16.3 %collective-permute-start.48 = (bf16[2,192,384]{2,1,0:T(8,128)(2,1)S(1)}, bf16[2,192,384]{2,1,0:T(8,128)(2,1)S(1)}, u32[]{:S(2)}, u32[]{:S(2)}) collective-permute-start(bf16[2,192,384]{2,1,0:T(8,128)(2,1)S(1)} %get-tuple-element.773), channel_id=1, source_target_pairs={{0,8},{1,9},{2,10},{3,11},{4,12},{5,13},{6,14},{7,15},{8,0},{9,1},... | collective-permute-start | bytes 884744 | tf_op jit(solution)/shard_map/ppermute | solution.py:385
  (40 other events, 330.5 us)
